TPU v7x, 128 devices: a whole 4x4x4 slice. The times are simulated.
128 devices in a mesh: section: 2 (over core), dp: 16 (over x, z), tensor: 4 (over y).
Axes of the slice: x: 4, y: 4, z: 4, core: 2. Of those that a mesh axis runs over, the one named last changes fastest.
Arguments:
- pipe_in: bfloat16 [2, 2, 4096, 1024], P('section', None, 'dp'), may hold values from -6 to 6
- doc_lengths: int32 [32, 4], P('dp'), may hold values from 1 to 128, 256 in all within a row
- norm_in: bfloat16 [2, 1024], P('section', ('dp', 'tensor')), may hold values from 0.5 to 1.5
- w_query: bfloat16 [2, 1024, 512], P('section', 'dp', 'tensor'), may hold values from -0.1875 to 0.1875
- w_key: bfloat16 [2, 1024, 512], P('section', 'dp', 'tensor'), may hold values from -0.1875 to 0.1875
- w_value: bfloat16 [2, 1024, 1024], P('section', 'dp', 'tensor'), may hold values from -0.1875 to 0.1875
- w_out_gate: bfloat16 [2, 1024, 1024], P('section', 'dp', 'tensor'), may hold values from -0.1875 to 0.1875
- w_rank_down: bfloat16 [2, 1024, 16], P('section', ('dp', 'tensor')), may hold values from -0.1875 to 0.1875
- w_rank_up: bfloat16 [2, 16, 512], P('section', 'dp', 'tensor'), may hold values from -1.5 to 1.5
- rank_bias: bfloat16 [2, 512], P('section', ('dp', 'tensor')), may hold values from -2 to 4
- head_gain: bfloat16 [2, 256], P('section', ('dp', 'tensor')), may hold values from 0.5 to 1.5
- w_out: bfloat16 [2, 1024, 1024], P('section', 'tensor', 'dp'), may hold values from -0.375 to 0.375
- norm_mid: bfloat16 [2, 1024], P('section', ('dp', 'tensor')), may hold values from 0.5 to 1.5
- w_gate: bfloat16 [2, 1024, 2816], P('section', 'dp', 'tensor'), may hold values from -0.1875 to 0.1875
- w_up: bfloat16 [2, 1024, 2816], P('section', 'dp', 'tensor'), may hold values from -0.1875 to 0.1875
- w_down: bfloat16 [2, 2816, 1024], P('section', 'tensor', 'dp'), may hold values from -0.21875 to 0.21875
Outputs:
- pipe_ends: float32 [2, 2, 4096, 1024], P('section', None, 'dp')
- grad_norm_in: float32 [2, 1024], P('section', ('dp', 'tensor'))
- grad_query: float32 [2, 1024, 512], P('section', 'dp', 'tensor')
- grad_key: float32 [2, 1024, 512], P('section', 'dp', 'tensor')
- grad_value: float32 [2, 1024, 1024], P('section', 'dp', 'tensor')
- grad_out_gate: float32 [2, 1024, 1024], P('section', 'dp', 'tensor')
- grad_rank_down: float32 [2, 1024, 16], P('section', ('dp', 'tensor'))
- grad_rank_up: float32 [2, 16, 512], P('section', 'dp', 'tensor')
- grad_rank_bias: float32 [2, 512], P('section', ('dp', 'tensor'))
- grad_head_gain: float32 [2, 256], P('section', ('dp', 'tensor'))
- grad_out: float32 [2, 1024, 1024], P('section', 'tensor', 'dp')
- grad_norm_mid: float32 [2, 1024], P('section', ('dp', 'tensor'))
- grad_gate: float32 [2, 1024, 2816], P('section', 'dp', 'tensor')
- grad_up: float32 [2, 1024, 2816], P('section', 'dp', 'tensor')
- grad_down: float32 [2, 2816, 1024], P('section', 'tensor', 'dp')
Inputs may be any that keep to these rules, and one draw needn't show every extreme that they name: `doc_lengths`: each row holds the lengths of 4 documents that fill one device's 256 tokens of one micro-batch exactly; the longest of every row is exactly 128.
All inputs are finite; a program needn't handle non-finite values.
Results may differ from a plain program's by a relative error of at most 0.03.
Values may be sent and summed in bfloat16 or wider, within the bound.
A program may use at most 192 MiB of HBM per device.

v0:
```python
import functools

import jax
import jax.numpy as jnp
from jax import lax
from jax.experimental import pallas as pl
from jax.experimental.pallas import tpu as pltpu
from jax.sharding import PartitionSpec as P

CH = 64
HK = 128
HV = 256
TOK = 256
BLOCKS = TOK // CH
FFD = 704
FFM = 640
QKVG = (0, 768)
OUT = (768, 256)
GU = (1024, 1408)
DOWN = (2432, 768)
WIDE = 3200
epsilon = 1e-06
head_floor = 1.0
MESH = pl.DeviceIdType.MESH
f32 = jnp.float32
bf16 = jnp.bfloat16

GATHER = (
    (0, 384, 0),
    (384, 384, 1),
    (768, 768, 0),
    (1536, 896, 1),
    (2432, 384, 0),
    (2816, 384, 1),
)
SCATTER = (
    (1024, 1408, 0),
    (2432, 768, 1),
    (768, 256, 0),
    (0, 384, 0),
    (384, 384, 1),
)


def dot(a, b):
    return lax.dot_general(a, b, (((1,), (0,)), ((), ())), preferred_element_type=f32)


def dot_back(a, b):
    return lax.dot_general(a, b, (((1,), (1,)), ((), ())), preferred_element_type=f32)


def dot_grad(a, b):
    return lax.dot_general(a, b, (((0,), (0,)), ((), ())), preferred_element_type=f32)


def low(a):
    return a.astype(bf16)


def wide(a):
    return a.astype(f32)


def rms_scale(v):
    return lax.rsqrt(jnp.mean(v * v, axis=-1, keepdims=True) + epsilon)


def kernel(
    X,
    Z,
    T,
    own,
    shard,
    norm_in,
    norm_mid,
    gain,
    bias,
    rank_down,
    rank_up,
    allowed,
    aux,
    ends,
    og,
    sg,
    W,
    xbuf,
    x1,
    normed,
    nm,
    qkvg,
    cum,
    slope,
    amat,
    states,
    attn,
    mixed,
    hid,
    gu,
    inner,
    rank,
    dh,
    dy0,
    res,
    res_in,
    pbuf,
    rbuf,
    G,
    GA,
    GB,
    GC,
    Q,
    RF,
    dqkvg,
    dmix,
    a_sem,
    gs,
    gr,
    ys,
    yr,
    ss,
    sr,
    e_sem,
):
    c = lax.axis_index("section")
    d = lax.axis_index("dp")
    t = lax.axis_index("tensor")
    x, z = d // Z, d % Z
    o = 1 - c
    D = own.shape[-1]
    R = shard.shape[0]
    H = R // 2
    TL = TOK // T
    size = (X, Z)
    here = (x, z)

    def dp_peer(axis, k):
        if axis == 0:
            return ((x + k) % X) * Z + z
        return x * Z + (z + k) % Z

    def remote(src, dst, s, r, **device):
        return pltpu.make_async_remote_copy(
            src_ref=src, dst_ref=dst, send_sem=s, recv_sem=r, device_id=device, device_id_type=MESH
        )

    barrier = pltpu.get_barrier_semaphore()
    for k in range(1, X):
        pl.semaphore_signal(barrier, inc=1, device_id={"dp": dp_peer(0, k)}, device_id_type=MESH)
    for k in range(1, Z):
        pl.semaphore_signal(barrier, inc=1, device_id={"dp": dp_peer(1, k)}, device_id_type=MESH)
    for k in range(1, T):
        pl.semaphore_signal(barrier, inc=1, device_id={"tensor": (t + k) % T}, device_id_type=MESH)
    pl.semaphore_signal(barrier, inc=1, device_id={"section": o}, device_id_type=MESH)
    pl.semaphore_wait(barrier, X + Z + T - 2)

    half = lambda h: pl.ds(pl.multiple_of(h * H, H), H)
    swap_w = remote(shard.at[half(o)], W.at[c, x, z, o], a_sem.at[0], a_sem.at[1], section=o)
    swap_x = remote(own.at[o], xbuf.at[c], a_sem.at[2], a_sem.at[3], section=o)
    keep_w = pltpu.make_async_copy(shard.at[half(c)], W.at[c, x, z, c], a_sem.at[4])
    keep_x = pltpu.make_async_copy(own.at[c], xbuf.at[c], a_sem.at[5])
    swap_w.start()
    swap_x.start()
    keep_w.start()
    keep_x.start()
    got_w = remote(shard.at[half(o)], W.at[o, x, z, c], a_sem.at[0], a_sem.at[1], section=o)
    got_x = remote(own.at[o], xbuf.at[o], a_sem.at[2], a_sem.at[3], section=o)

    def w_first(l, j, k):
        c0, n, axis = GATHER[j]
        at = W.at[l, x, z, c, :, pl.ds(c0, n)]
        if axis == 0:
            into = W.at[l, (x - k) % X, z, c, :, pl.ds(c0, n)]
        else:
            into = W.at[l, x, (z - k) % Z, c, :, pl.ds(c0, n)]
        s, r = gs.at[l, j, k - 1], gr.at[l, j, k - 1]
        return remote(at, at, s, r, dp=dp_peer(axis, k)), remote(into, into, s, r, dp=dp_peer(axis, k))

    def w_second(l, j, k):
        c0, n, axis = GATHER[j]
        cols = pl.ds(c0, n)
        if axis == 0:
            at, into = W.at[l, :, z, c, :, cols], W.at[l, :, (z - k) % Z, c, :, cols]
        else:
            at, into = W.at[l, x, :, c, :, cols], W.at[l, (x - k) % X, :, c, :, cols]
        s, r = gs.at[l, j, 2 + k], gr.at[l, j, 2 + k]
        return remote(at, at, s, r, dp=dp_peer(1 - axis, k)), remote(
            into, into, s, r, dp=dp_peer(1 - axis, k)
        )

    def w_third(l, j):
        c0, n, _ = GATHER[j]
        cols = pl.ds(c0, n)
        at, into = W.at[l, :, :, c, :, cols], W.at[l, :, :, o, :, cols]
        s, r = gs.at[l, j, 6], gr.at[l, j, 6]
        return remote(at, at, s, r, section=o), remote(into, into, s, r, section=o)

    def gather_first(l, j):
        for k in range(1, size[GATHER[j][2]]):
            w_first(l, j, k)[0].start()

    def gather_second(l, j):
        axis = GATHER[j][2]
        for k in range(1, size[axis]):
            w_first(l, j, k)[1].wait_recv()
        for k in range(1, size[1 - axis]):
            w_second(l, j, k)[0].start()

    def gather_third(l, j):
        axis = GATHER[j][2]
        for k in range(1, size[1 - axis]):
            w_second(l, j, k)[1].wait_recv()
        w_third(l, j)[0].start()

    arrived = set()

    def weight(l, part):
        c0, n = part
        for j, (g0, gn, _) in enumerate(GATHER):
            if g0 < c0 + n and c0 < g0 + gn and (l, j) not in arrived:
                arrived.add((l, j))
                w_third(l, j)[1].wait_recv()
        return W[l, :, :, :, :, c0 : c0 + n].reshape(D, n)

    def rows(p):
        return pl.ds(pl.multiple_of(p * TL, TL), TL)

    def sum_copy(i, k):
        peer = (t + k) % T
        return remote(
            pbuf.at[i // 2 % 2, rows(peer)], rbuf.at[i // 2 % 2, k - 1], ys.at[i, k - 1], yr.at[i, k - 1], tensor=peer
        )

    def sum_start(i, part):
        pbuf[i // 2 % 2] = low(part)
        for k in range(1, T):
            sum_copy(i, k).start()

    def sum_wait(i):
        total = wide(pbuf[i // 2 % 2, rows(t)])
        for k in range(1, T):
            sum_copy(i, k).wait_recv()
            total = total + wide(rbuf[i // 2 % 2, k - 1])
        for k in range(1, T):
            sum_copy(i, k).wait_send()
        return total

    def share_copy(i, ref, k):
        peer = (t + k) % T
        s, r = ys.at[i, k - 1], yr.at[i, k - 1]
        mine, into = ref.at[rows(t)], ref.at[rows((t - k) % T)]
        return remote(mine, mine, s, r, tensor=peer), remote(into, into, s, r, tensor=peer)

    def share_start(i, ref, value):
        ref[rows(t)] = low(value)
        for k in range(1, T):
            share_copy(i, ref, k)[0].start()

    def share_wait(i, ref):
        for k in range(1, T):
            share_copy(i, ref, k)[1].wait_recv()
        for k in range(1, T):
            share_copy(i, ref, k)[0].wait_send()

    def s_swap(l, j):
        c0, n, _ = SCATTER[j]
        cols = pl.ds(c0, n)
        return remote(
            G.at[:, :, o, :, cols], GA.at[l, :, :, :, cols], ss.at[l, j, 0], sr.at[l, j, 0], section=o
        )

    def s_first(l, j, k):
        c0, n, axis = SCATTER[j]
        cols = pl.ds(c0, n)
        src = G.at[(x + k) % X, :, c, :, cols] if axis == 0 else G.at[:, (z + k) % Z, c, :, cols]
        return remote(
            src, GB.at[l, k - 1, :, :, cols], ss.at[l, j, k], sr.at[l, j, k], dp=dp_peer(axis, k)
        )

    def s_second(l, j, k):
        c0, n, axis = SCATTER[j]
        cols = pl.ds(c0, n)
        place = (here[1 - axis] + k) % size[1 - axis]
        return remote(
            Q.at[l, place, :, cols],
            GC.at[l, k - 1, :, cols],
            ss.at[l, j, 3 + k],
            sr.at[l, j, 3 + k],
            dp=dp_peer(1 - axis, k),
        )

    def scatter_swap(l, j):
        s_swap(l, j).start()

    def scatter_first(l, j):
        c0, n, axis = SCATTER[j]
        s_swap(l, j).wait()
        for a in range(X):
            G[a, :, c, :, c0 : c0 + n] = low(
                wide(G[a, :, c, :, c0 : c0 + n]) + wide(GA[l, a, :, :, c0 : c0 + n])
            )
        for k in range(1, size[axis]):
            s_first(l, j, k).start()

    def scatter_second(l, j):
        c0, n, axis = SCATTER[j]
        cols = slice(c0, c0 + n)
        total = wide(G[x, :, c, :, cols] if axis == 0 else G[:, z, c, :, cols])
        for k in range(1, size[axis]):
            s_first(l, j, k).wait()
            total = total + wide(GB[l, k - 1, :, :, cols])
        Q[l, :, :, cols] = low(total)
        for k in range(1, size[1 - axis]):
            s_second(l, j, k).start()

    def scatter_third(l, j):
        c0, n, axis = SCATTER[j]
        cols = slice(c0, c0 + n)
        total = wide(Q[l, here[1 - axis], :, cols])
        for k in range(1, size[1 - axis]):
            s_second(l, j, k).wait()
            total = total + wide(GC[l, k - 1, :, cols])
        RF[l, :, cols] = total

    scale = HK**-0.5
    sub = lambda v, n: v[n * CH : (n + 1) * CH]

    def mixer_forward(l):
        qk = qkvg[l]
        b = cum[l]
        qd = low(qk[:, 0:128] * scale * jnp.exp(b))
        kd = low(qk[:, 128:256] * jnp.exp(-b))
        v = low(qk[:, 256:512])
        scores = low(jnp.where(allowed[...] > 0.0, dot_back(qd, kd), 0.0))
        amat[l] = scores
        within = dot(scores, v)
        out = [sub(within, 0)]
        state = None
        for n in range(BLOCKS - 1):
            bn = sub(b, n)
            last = bn[CH - 1 : CH]
            tail = sub(aux[...], n)[:, 1:2]
            kt = low(sub(qk, n)[:, 128:256] * jnp.exp(last - bn) * tail)
            fresh = dot_grad(sub(v, n), kt)
            if state is None:
                state = fresh
            else:
                state = aux[n * CH : n * CH + 1, 2:3] * jnp.exp(last) * state + fresh
            states[l, n] = state
            carried = sub(aux[...], n + 1)[:, 0:1]
            out.append(sub(within, n + 1) + carried * dot_back(sub(qd, n + 1), low(state)))
        attn[l] = jnp.concatenate(out, axis=0)

    def running(v, upper):
        row = lax.broadcasted_iota(jnp.int32, (TOK, TOK), 0)
        col = lax.broadcasted_iota(jnp.int32, (TOK, TOK), 1)
        order = (row <= col) if upper else (row >= col)
        tri = jnp.where(jnp.logical_and(order, row // CH == col // CH), 1.0, 0.0).astype(bf16)
        first = low(v)
        rest = v - wide(first)
        second = low(rest)
        third = low(rest - wide(second))
        return dot(tri, first) + (dot(tri, second) + dot(tri, third))

    def forward(l, i, x_ref, out_ref, hooks):
        xin = wide(x_ref[...])
        normed[l] = low(xin * rms_scale(xin) * norm_in[l])
        hooks[0]()
        nrm = normed[l]
        qkvg[l] = dot(nrm, weight(l, QKVG))
        rank[l] = low(dot(nrm, rank_down[l]))
        pre = dot(rank[l], rank_up[l]) + bias[l]
        soft = jnp.log1p(jnp.exp(-jnp.abs(pre)))
        slope[l] = jax.nn.sigmoid(-pre) / 16.0
        cum[l] = running((jnp.minimum(pre, 0.0) - soft) / 16.0, False)
        mixer_forward(l)
        at = attn[l]
        g = qkvg[l, :, 512:768]
        head = lax.rsqrt(jnp.mean(at * at, axis=-1, keepdims=True) + head_floor)
        mixed[l] = low(at * head * gain[l] * g * jax.nn.sigmoid(g))
        sum_start(i, dot_back(mixed[l], weight(l, OUT)))
        hooks[1]()
        hidden = wide(x_ref[rows(t)]) + sum_wait(i)
        hid[l] = hidden
        share_start(i + 1, nm.at[l], hidden * rms_scale(hidden) * norm_mid[l])
        hooks[2]()
        w_gu = weight(l, GU)
        share_wait(i + 1, nm.at[l])
        acts = dot(nm[l], w_gu)
        gu[l] = acts
        first = jax.nn.silu(acts[:, :FFM]) * acts[:, FFM : 2 * FFM]
        both = acts[:, 2 * FFM :]
        lane = lax.broadcasted_iota(jnp.int32, (TOK, 128), 1)
        last = jnp.where(lane < 64, jax.nn.silu(both) * pltpu.roll(both, 64, 1), 0.0)
        inner[l, :, :FFM] = low(first)
        inner[l, :, FFM:] = low(last)
        sum_start(i + 2, dot_back(inner[l], weight(l, DOWN)))
        hooks[3]()
        y = hid[l] + sum_wait(i + 2)
        share_start(i + 3, out_ref, y)

    def silu_parts(v):
        sig = jax.nn.sigmoid(v)
        return v * sig, sig * (1.0 + v * (1.0 - sig))

    def put(part, left, right):
        c0, n = part
        step = D // X
        for a in range(X):
            G[a, :, :, :, c0 : c0 + n] = low(
                dot_grad(left[:, a * step : (a + 1) * step], right)
            ).reshape(Z, 2, H, n)

    def mixer_backward(l):
        at = attn[l]
        g = qkvg[l, :, 512:768]
        head = lax.rsqrt(jnp.mean(at * at, axis=-1, keepdims=True) + head_floor)
        unit = at * head
        act, act_slope = silu_parts(g)
        dm = dmix[...]
        dqkvg[:, 512:768] = low(dm * unit * gain[l] * act_slope)
        du = dm * act
        d_gain = jnp.sum(du * unit, axis=0, keepdims=True)
        w = du * gain[l]
        do = low(head * (w - unit * jnp.mean(w * unit, axis=-1, keepdims=True)))
        q, k = qkvg[l, :, 0:128], qkvg[l, :, 128:256]
        b = cum[l]
        grow, shrink = jnp.exp(b), jnp.exp(-b)
        qd = low(q * scale * grow)
        kd = low(k * shrink)
        v = low(qkvg[l, :, 256:512])
        d_scores = low(jnp.where(allowed[...] > 0.0, dot_back(do, v), 0.0))
        d_qd = dot(d_scores, kd)
        d_kd = dot_grad(d_scores, qd)
        d_v = dot_grad(amat[l], do)
        d_b = wide(qd) * d_qd - wide(kd) * d_kd
        d_k = d_kd * shrink
        out_q, out_k, out_v, out_b = [None] * BLOCKS, [None] * BLOCKS, [None] * BLOCKS, [None] * BLOCKS
        d_state = None
        for n in reversed(range(BLOCKS)):
            dq_n, dk_n, dv_n, db_n = sub(d_qd, n), sub(d_k, n), sub(d_v, n), sub(d_b, n)
            if n < BLOCKS - 1:
                bn = sub(b, n)
                last = bn[CH - 1 : CH]
                fade = jnp.exp(last - bn) * sub(aux[...], n)[:, 1:2]
                kt = low(sub(k, n) * fade)
                d_low = low(d_state)
                d_kt = dot(sub(v, n), d_low)
                dv_n = dv_n + dot_back(kt, d_low)
                dk_n = dk_n + d_kt * fade
                moved = wide(kt) * d_kt
                db_n = db_n - moved
                d_last = jnp.sum(moved, axis=0, keepdims=True)
                if n > 0:
                    keep = aux[n * CH : n * CH + 1, 2:3] * jnp.exp(last)
                    d_last = d_last + keep * jnp.sum(
                        states[l, n - 1] * d_state, axis=0, keepdims=True
                    )
                place = lax.broadcasted_iota(jnp.int32, (CH, HK), 0)
                db_n = db_n + jnp.where(place == CH - 1, d_last, 0.0)
            if n > 0:
                do_n = low(wide(sub(do, n)) * sub(aux[...], n)[:, 0:1])
                d_across = dot(do_n, low(states[l, n - 1]))
                dq_n = dq_n + d_across
                db_n = db_n + wide(sub(qd, n)) * d_across
                fresh = dot_grad(do_n, sub(qd, n))
                d_state = fresh if n == BLOCKS - 1 else keep * d_state + fresh
            out_q[n], out_k[n], out_v[n], out_b[n] = dq_n, dk_n, dv_n, db_n
        dqkvg[:, 0:128] = low(jnp.concatenate(out_q, axis=0) * scale * grow)
        dqkvg[:, 128:256] = low(jnp.concatenate(out_k, axis=0))
        dqkvg[:, 256:512] = low(jnp.concatenate(out_v, axis=0))
        d_decay = running(jnp.concatenate(out_b, axis=0), True)
        return low(d_decay * slope[l]), d_gain

    def backward(l, i, x_ref, dy_ref, out_ref, hooks):
        dy = dy_ref[...]
        d_inner = dot(dy, weight(l, DOWN))
        gate, up, both = gu[l, :, :FFM], gu[l, :, FFM : 2 * FFM], gu[l, :, 2 * FFM :]
        act, act_slope = silu_parts(gate)
        act_b, slope_b = silu_parts(both)
        rest = d_inner[:, FFM:]
        mix_b = rest * pltpu.roll(both, 64, 1) * slope_b + pltpu.roll(rest * act_b, 64, 1)
        d_gu = jnp.concatenate(
            [low(d_inner[:, :FFM] * up * act_slope), low(d_inner[:, :FFM] * act), low(mix_b)], axis=1
        )
        sum_start(i, dot_back(d_gu, weight(l, GU)))
        put(DOWN, dy, inner[l])
        scatter_swap(l, 1)
        put(GU, nm[l], d_gu)
        scatter_swap(l, 0)
        hooks[0]()
        d_mid = sum_wait(i)
        hidden = hid[l]
        scale_mid = rms_scale(hidden)
        unit = hidden * scale_mid
        sg[l, 17:18, :] = jnp.sum(d_mid * unit, axis=0, keepdims=True)
        scaled = d_mid * norm_mid[l]
        d_hidden = wide(dy_ref[rows(t)]) + scale_mid * (
            scaled - unit * jnp.mean(scaled * unit, axis=-1, keepdims=True)
        )
        hid[l] = d_hidden
        share_start(i + 1, dh.at[l], d_hidden)
        hooks[1]()
        share_wait(i + 1, dh.at[l])
        dmix[...] = dot(dh[l], weight(l, OUT))
        d_pre, d_gain = mixer_backward(l)
        d_rank = low(dot_back(d_pre, rank_up[l]))
        sum_start(i + 2, dot_back(dqkvg[...], weight(l, QKVG)) + dot_back(d_rank, rank_down[l]))
        hooks[2]()
        put(OUT, dh[l], mixed[l])
        scatter_swap(l, 2)
        put(QKVG, normed[l], dqkvg[...])
        scatter_swap(l, 3)
        scatter_swap(l, 4)
        sg[l, 0:16, :] = dot_grad(d_rank, normed[l])[0:16]
        sg[l, 18:19, 0:HV] = d_gain
        sg[l, 19:20, 0:HK] = jnp.sum(wide(d_pre), axis=0, keepdims=True)
        sg[l, 24:40, 0:HK] = dot_grad(rank[l], d_pre)[0:16]
        hooks[3]()
        d_normed = sum_wait(i + 2)
        xin = wide(x_ref[rows(t)])
        scale_in = rms_scale(xin)
        unit = xin * scale_in
        sg[l, 16:17, :] = jnp.sum(d_normed * unit, axis=0, keepdims=True)
        scaled = d_normed * norm_in[l]
        dx = hid[l] + scale_in * (scaled - unit * jnp.mean(scaled * unit, axis=-1, keepdims=True))
        share_start(i + 3, out_ref, dx)

    def nothing():
        pass

    count = len(GATHER)

    def first_weights():
        got_w.wait_recv()
        keep_w.wait()
        for j in range(count):
            gather_first(0, j)
        for j in range(count):
            gather_second(0, j)
        for j in range(count):
            gather_third(0, j)
        for j in range(count):
            gather_first(1, j)

    def each(step, l, which):
        def run():
            for j in which:
                step(l, j)

        return run

    sg[...] = jnp.zeros_like(sg)
    got_x.wait_recv()
    keep_x.wait()
    everything = range(count)
    forward(
        0,
        0,
        xbuf.at[0],
        x1,
        (first_weights, each(gather_second, 1, everything), nothing, each(gather_third, 1, everything)),
    )
    share_wait(3, x1)
    forward(1, 4, x1, res.at[1], (nothing, nothing, nothing, nothing))

    def send_y():
        share_wait(7, res.at[1])

    ff, mix = (0, 1), (2, 3, 4)
    backward(
        1,
        8,
        x1,
        xbuf.at[1],
        dy0,
        (
            send_y,
            each(scatter_first, 1, ff),
            each(scatter_second, 1, ff),
            each(scatter_third, 1, ff),
        ),
    )
    each(scatter_first, 1, mix)()
    share_wait(11, dy0)

    def in_second():
        each(scatter_first, 0, ff)()
        each(scatter_third, 1, mix)()

    backward(
        0,
        12,
        xbuf.at[0],
        dy0,
        res.at[0],
        (each(scatter_second, 1, mix), in_second, each(scatter_second, 0, ff), each(scatter_third, 0, ff)),
    )
    each(scatter_first, 0, mix)()
    share_wait(15, res.at[0])
    give_end = remote(res.at[o], res_in, e_sem.at[0], e_sem.at[1], section=o)
    give_end.start()
    each(scatter_second, 0, mix)()
    ends[c] = wide(res[c])
    each(scatter_third, 0, mix)()
    give_grad = remote(RF.at[o], og.at[c], e_sem.at[2], e_sem.at[3], section=o)
    got_grad = remote(RF.at[o], og.at[o], e_sem.at[2], e_sem.at[3], section=o)
    give_grad.start()
    og[c] = RF[c]
    give_end.wait_recv()
    ends[o] = wide(res_in[...])
    got_grad.wait_recv()
    give_end.wait_send()
    give_grad.wait_send()
    swap_w.wait_send()
    swap_x.wait_send()
    for l in range(2):
        for j, (_, _, axis) in enumerate(GATHER):
            for k in range(1, size[axis]):
                w_first(l, j, k)[0].wait_send()
            for k in range(1, size[1 - axis]):
                w_second(l, j, k)[0].wait_send()
            w_third(l, j)[0].wait_send()


def run_kernel(X, Z, T, D, R, operands):
    H = R // 2
    TL = TOK // T
    top = max(X, Z)
    scratch = [
        pltpu.VMEM((2, X, Z, 2, H, WIDE), bf16),
        pltpu.VMEM((2, TOK, D), bf16),
        pltpu.VMEM((TOK, D), bf16),
        pltpu.VMEM((2, TOK, D), bf16),
        pltpu.VMEM((2, TOK, D), bf16),
        pltpu.VMEM((2, TOK, 768), f32),
        pltpu.VMEM((2, TOK, HK), f32),
        pltpu.VMEM((2, TOK, HK), f32),
        pltpu.VMEM((2, TOK, TOK), bf16),
        pltpu.VMEM((2, BLOCKS - 1, HV, HK), f32),
        pltpu.VMEM((2, TOK, HV), f32),
        pltpu.VMEM((2, TOK, HV), bf16),
        pltpu.VMEM((2, TL, D), f32),
        pltpu.VMEM((2, TOK, GU[1]), f32),
        pltpu.VMEM((2, TOK, DOWN[1]), bf16),
        pltpu.VMEM((2, TOK, 128), bf16),
        pltpu.VMEM((2, TOK, D), bf16),
        pltpu.VMEM((TOK, D), bf16),
        pltpu.VMEM((2, TOK, D), bf16),
        pltpu.VMEM((TOK, D), bf16),
        pltpu.VMEM((2, TOK, D), bf16),
        pltpu.VMEM((2, T - 1, TL, D), bf16),
        pltpu.VMEM((X, Z, 2, H, WIDE), bf16),
        pltpu.VMEM((2, X, Z, H, WIDE), bf16),
        pltpu.VMEM((2, top - 1, top, H, WIDE), bf16),
        pltpu.VMEM((2, top - 1, H, WIDE), bf16),
        pltpu.VMEM((2, top, H, WIDE), bf16),
        pltpu.VMEM((2, H, WIDE), f32),
        pltpu.VMEM((TOK, 768), bf16),
        pltpu.VMEM((TOK, HV), f32),
        pltpu.SemaphoreType.DMA((6,)),
        pltpu.SemaphoreType.DMA((2, len(GATHER), 7)),
        pltpu.SemaphoreType.DMA((2, len(GATHER), 7)),
        pltpu.SemaphoreType.DMA((16, T - 1)),
        pltpu.SemaphoreType.DMA((16, T - 1)),
        pltpu.SemaphoreType.DMA((2, len(SCATTER), 7)),
        pltpu.SemaphoreType.DMA((2, len(SCATTER), 7)),
        pltpu.SemaphoreType.DMA((4,)),
    ]
    vmem = pl.BlockSpec(memory_space=pltpu.VMEM)
    return pl.pallas_call(
        functools.partial(kernel, X, Z, T),
        out_shape=(
            jax.ShapeDtypeStruct((2, TOK, D), f32),
            jax.ShapeDtypeStruct((2, H, WIDE), f32),
            jax.ShapeDtypeStruct((2, 40, D), f32),
        ),
        in_specs=[vmem] * len(operands),
        out_specs=(vmem,) * 3,
        scratch_shapes=scratch,
        compiler_params=pltpu.CompilerParams(
            collective_id=0, has_side_effects=True, vmem_limit_bytes=63 * 1024 * 1024
        ),
    )(*operands)


def mask_arrays(lengths):
    bounds = jnp.cumsum(lengths)
    places = jnp.arange(TOK, dtype=jnp.int32)
    seg = jnp.sum((bounds[None, :] <= places[:, None]).astype(jnp.int32), axis=1)
    by_block = seg.reshape(BLOCKS, CH)
    last = by_block[:, CH - 1]
    before = jnp.concatenate([jnp.full((1,), -1, jnp.int32), last[:-1]])
    carried = (by_block == before[:, None]).reshape(TOK).astype(f32)
    tail = (by_block == last[:, None]).reshape(TOK).astype(f32)
    retain = jnp.broadcast_to((last == before)[:, None], (BLOCKS, CH)).reshape(TOK).astype(f32)
    block = places // CH
    allowed = (
        (places[:, None] >= places[None, :])
        & (block[:, None] == block[None, :])
        & (seg[:, None] == seg[None, :])
    ).astype(f32)
    aux = jnp.pad(jnp.stack([carried, tail, retain], axis=1), ((0, 0), (0, 125)))
    return allowed, aux


def on_device(
    X,
    Z,
    pipe_in,
    doc_lengths,
    norm_in,
    w_query,
    w_key,
    w_value,
    w_out_gate,
    w_rank_down,
    w_rank_up,
    rank_bias,
    head_gain,
    w_out,
    norm_mid,
    w_gate,
    w_up,
    w_down,
):
    T = lax.axis_size("tensor")
    N = X * Z
    c = lax.axis_index("section")
    d = lax.axis_index("dp")
    t = lax.axis_index("tensor")
    R = w_query.shape[1]
    D = R * N
    shard = jnp.concatenate(
        [
            w_query[0],
            w_key[0],
            w_value[0],
            w_out_gate[0],
            w_out[0].T,
            w_gate[0, :, :FFM],
            w_up[0, :, :FFM],
            w_gate[0, :, FFM:],
            w_up[0, :, FFM:],
            w_down[0].T,
            jnp.zeros((R, 2 * FFM + 128 - 2 * FFD + DOWN[1] - FFD), bf16),
        ],
        axis=1,
    )
    mine = [norm_in[0], norm_mid[0], head_gain[0], rank_bias[0], w_rank_down[0].reshape(-1), w_rank_up[0, 0]]
    widths = [a.shape[0] for a in mine]
    smalls = lax.all_gather(jnp.concatenate(mine), ("section", "dp", "tensor"), axis=0, tiled=False)
    smalls = smalls.reshape(2, N, T, -1)
    parts, at = [], 0
    for w in widths:
        parts.append(smalls[..., at : at + w])
        at += w
    g_in = parts[0].reshape(2, 1, D).astype(f32)
    g_mid = parts[1].reshape(2, 1, D).astype(f32)
    g_head = parts[2].reshape(2, 1, HV).astype(f32)
    bias = lax.dynamic_slice_in_dim(parts[3].reshape(2, 1, T * HK).astype(f32), t * HK, HK, 2)
    G = w_rank_down.shape[2]
    down = jnp.pad(parts[4].reshape(2, D, G), ((0, 0), (0, 0), (0, 128 - G)))
    up = lax.dynamic_index_in_dim(parts[5], t, 2, keepdims=False)
    up = jnp.pad(up, ((0, 0), (0, 128 - N), (0, 0)))
    allowed, aux = mask_arrays(lax.dynamic_index_in_dim(doc_lengths, c, 0, keepdims=False))
    operands = (pipe_in[0], shard, g_in, g_mid, g_head, bias, down, up, allowed, aux)
    ends, og, sg = run_kernel(X, Z, T, D, R, operands)
    og = og.reshape(R, WIDE)
    head = jnp.zeros((2, 1, T * HK), f32)
    head = lax.dynamic_update_slice_in_dim(head, sg[:, 19:20, 0:HK], t * HK, 2)
    ups = jnp.zeros((2, T, N * HK), f32)
    ups = lax.dynamic_update_slice_in_dim(ups, sg[:, 24 : 24 + N, 0:HK].reshape(2, 1, N * HK), t, 1)
    flat = jnp.concatenate(
        [sg[:, 0:18].reshape(2, -1), sg[:, 18, 0:HV], head.reshape(2, -1), ups.reshape(2, -1)], axis=1
    )
    flat = lax.psum(flat, ("section", "dp", "tensor"))
    flat = lax.dynamic_index_in_dim(flat, c, 0, keepdims=False)
    place = d * T + t
    block = D // (N * T)
    table = flat[: 18 * D].reshape(18, D)
    table = lax.dynamic_slice_in_dim(table, place * block, block, 1)
    at = 18 * D
    o_gain = lax.dynamic_slice_in_dim(flat[at : at + HV], place * (HV // (N * T)), HV // (N * T), 0)
    at += HV
    o_bias = lax.dynamic_slice_in_dim(
        flat[at : at + T * HK], place * (T * HK // (N * T)), T * HK // (N * T), 0
    )
    at += T * HK
    o_up = lax.dynamic_index_in_dim(flat[at:].reshape(T, N, HK), t, 0, keepdims=False)
    o_up = lax.dynamic_slice_in_dim(o_up, d, 1, 0)
    gates = og[:, GU[0] : GU[0] + GU[1]]
    return (
        ends[None],
        table[16][None],
        og[None, :, 0:128],
        og[None, :, 128:256],
        og[None, :, 256:512],
        og[None, :, 512:768],
        table[0:G].T[None],
        o_up[None],
        o_bias[None],
        o_gain[None],
        og[:, OUT[0] : OUT[0] + OUT[1]].T[None],
        table[17][None],
        jnp.concatenate([gates[:, :FFM], gates[:, 2 * FFM : 2 * FFM + 64]], axis=1)[None],
        jnp.concatenate([gates[:, FFM : 2 * FFM], gates[:, 2 * FFM + 64 :]], axis=1)[None],
        og[:, DOWN[0] : DOWN[0] + FFD].T[None],
    )


def solution(mesh):
    count = mesh.shape["dp"]
    side = {16: 4, 4: 2}[count]
    in_specs = (
        P("section", None, "dp", None),
        P("dp", None),
        P("section", ("dp", "tensor")),
        P("section", "dp", "tensor"),
        P("section", "dp", "tensor"),
        P("section", "dp", "tensor"),
        P("section", "dp", "tensor"),
        P("section", ("dp", "tensor"), None),
        P("section", "dp", "tensor"),
        P("section", ("dp", "tensor")),
        P("section", ("dp", "tensor")),
        P("section", "tensor", "dp"),
        P("section", ("dp", "tensor")),
        P("section", "dp", "tensor"),
        P("section", "dp", "tensor"),
        P("section", "tensor", "dp"),
    )
    out_specs = (
        P("section", None, "dp", None),
        P("section", ("dp", "tensor")),
        P("section", "dp", "tensor"),
        P("section", "dp", "tensor"),
        P("section", "dp", "tensor"),
        P("section", "dp", "tensor"),
        P("section", ("dp", "tensor"), None),
        P("section", "dp", "tensor"),
        P("section", ("dp", "tensor")),
        P("section", ("dp", "tensor")),
        P("section", "tensor", "dp"),
        P("section", ("dp", "tensor")),
        P("section", "dp", "tensor"),
        P("section", "dp", "tensor"),
        P("section", "tensor", "dp"),
    )
    return jax.shard_map(
        functools.partial(on_device, side, count // side),
        mesh=mesh,
        in_specs=in_specs,
        out_specs=out_specs,
        check_vma=False,
    )
```

profile of v0, /device:TPU:1, one launch (start us, length us, event | category | flops | bytes accessed | tf_op | source)
XLA Modules:
  0.0 516.0 jit_solution(1065745670380305085)
XLA Ops:
  7.2 0.8 reshape_squeeze.3
  8.0 3.4 concatenate.22
  11.5 0.3 dynamic-update-slice
  11.7 0.6 copy-done.2
  12.4 0.9 slice_bitcast_fusion.2
  13.4 0.7 slice_bitcast_fusion.9
  14.1 0.2 reduce-window.8
  14.3 0.1 convert_reduce_fusion
  14.4 0.1 reshape.247
  14.5 0.2 slice_reduce_fusion.1
  14.7 0.2 slice_reduce_fusion
  14.9 0.8 fusion.2.allowed
  15.7 0.2 convert_reduce_fusion.1
  15.9 0.1 broadcast_in_dim.58
  16.0 0.1 convert_element_type.92
  16.1 0.1 pad_add_fusion
  16.1 0.1 eq.74
  16.2 0.1 eq.75
  16.3 0.1 eq.78
  16.4 0.1 eq.79
  16.5 0.1 copy.69
  16.6 0.7 pad.14.aux
  17.3 1.8 concatenate.21.shard
  19.1 136.7 %all-reduce.9.cloned.1.call-done = bf16[54784]{0:T(1024)(128)(2,1)} async-done(((bf16[54784]{0:T(1024)(128)(2,1)}), bf16[54784]{0:T(1024)(128)(2,1)}) %all-reduce.9.cloned.1.call-update) | async-done | bytes 109584
  155.9 1.2 reshape.243
  157.0 0.1 slice_convert_fusion.2
  157.1 0.1 slice_convert_fusion.1
  157.2 0.1 slice_convert_fusion
  157.3 0.1 slice.150
  157.4 0.1 slice.151
  157.5 0.7 reshape.255.norm_in
  158.2 0.7 reshape.256.norm_mid
  158.9 0.7 reshape.264.gain
  159.6 0.1 reshape.265
  159.8 0.4 reshape.244
  160.1 0.9 pad.12.rank_down
  161.1 0.6 pad.13.rank_up
  161.7 0.6 constant_dynamic-slice_fusion.4.bias
  162.3 189.5 %shard_map.271 = (f32[2,256,1024]{2,1,0:T(8,128)}, f32[2,32,3200]{2,1,0:T(8,128)}, f32[2,40,1024]{2,1,0:T(8,128)}) custom-call(bf16[2,256,1024]{2,1,0:T(8,128)(2,1)} %bitcast.68, bf16[64,3200]{1,0:T(8,128)(2,1)} %concatenate.21.shard, f32[2,1,1024]{2,1,0:T(1,128)} %reshape.255.norm_in, f32[2,1,1024]{2,1,0:T(1,128)} %reshape.256.norm_mid, ...), custom_call_target="tpu_custom_call" | custom-call | tf_op jit(solution)/shard_map/pallas_call | solution.py:671
  351.8 0.7 slice.128
  352.5 0.7 slice.127
  353.2 0.7 slice.126
  353.9 0.9 slice_bitcast_fusion.1
  354.9 1.6 slice_bitcast_fusion.7
  356.4 1.6 slice_bitcast_fusion.4
  358.0 0.9 fusion.5
  358.9 1.0 fusion.4
  359.9 1.6 slice_bitcast_fusion
  361.6 0.2 dynamic_update_slice.8
  361.7 0.1 copy.82
  361.8 0.1 copy.81
  361.9 0.8 pad_maximum_fusion
  362.8 0.7 maximum_bitcast_fusion
  363.4 0.7 maximum_bitcast_fusion.1
  364.1 137.2 %all-reduce.7.cloned.1.call-done = f32[2,27392]{1,0:T(2,128)} async-done(((f32[2,27392]{1,0:T(2,128)}), f32[2,27392]{1,0:T(2,128)}) %all-reduce.7.cloned.1.call-update) | async-done | bytes 219152 | tf_op jit(solution)/shard_map/psum | solution.py:777
  501.4 1.1 dynamic-slice_reduce_fusion
  502.5 0.1 constant_dynamic-slice_fusion
  502.6 0.7 copy.79
  503.3 0.6 fusion.6
  503.9 1.0 dynamic-slice.7
  504.8 0.5 constant_dynamic-slice_fusion.1
  505.4 1.2 dynamic-slice.9
  506.6 1.2 dynamic-slice.11
  507.9 1.3 copy.93
  (22 shorter events, 0.2 us)
Async XLA Ops:
  7.2 7.0 %copy-start = (s32[2,4]{1,0:T(2,128)S(1)}, s32[2,4]{1,0:T(2,128)}, u32[]{:S(2)}) copy-start(s32[2,4]{1,0:T(2,128)} %param.17) | copy-start | bytes 100
  7.2 148.7 %all-reduce.9.cloned.1.call-start = ((), (), s32[]{:S(2)}) async-start(), calls=%async_computation.1 | async-start | bytes 221184
  11.7 0.6 copy-start.2
  12.4 489.0 %all-reduce.7.cloned.1.call-start = ((), (), s32[]{:S(2)}) async-start(), calls=%async_computation | async-start | bytes 438272 | tf_op jit(solution)/shard_map/psum | solution.py:777
  354.8 153.0 %copy-start.1 = (f32[2,256,1024]{2,1,0:T(8,128)S(1)}, f32[2,256,1024]{2,1,0:T(8,128)}, u32[]{:S(2)}) copy-start(f32[2,256,1024]{2,1,0:T(8,128)} %get-tuple-element.18) | copy-start | bytes 6291460
Sparse Core Ops, SparseCore 0:
  13.3 142.4 all-reduce.8
  362.9 138.4 all-reduce.6
where the time goes:
time: 517 us; the launch traced here: 516 us
  waiting for transfers between devices  274 us (53%)
  Pallas kernels  189 us (37%)
  local copies, waits for them, and re-layouts  34.4 us (7%)
  between operations  14.3 us (3%)
    pallas_call x1, Pallas kernels, run_kernel(): pl.pallas_call(functools.partial(kernel, X, Z, T), out_shape=(jax.ShapeDt...  189 us
    psum x1, waiting for transfers between devices, on_device(): flat = lax.psum(flat, ('section', 'dp', 'tensor'))  137 us
    unnamed x3, waiting for transfers between devices  137 us
  transfers between devices with their start and end apart: 2, of which 2 were waited for; matrix products, arithmetic and copies ran while one was open for 2% of the time, Pallas kernels for 0%

commit v1 on v0

--- a/solution.py
+++ b/solution.py
@@ -18,7 +18,9 @@
 OUT = (768, 256)
 GU = (1024, 1408)
 DOWN = (2432, 768)
-WIDE = 3200
+SMALL = (3200, 128)
+WIDE = 3328
+AT_IN, AT_MID, AT_GAIN, AT_BIAS = 16, 17, 18, 19
 epsilon = 1e-06
 head_floor = 1.0
 MESH = pl.DeviceIdType.MESH
@@ -32,6 +34,7 @@
     (1536, 896, 1),
     (2432, 384, 0),
     (2816, 384, 1),
+    (3200, 128, 0),
 )
 SCATTER = (
     (1024, 1408, 0),
@@ -70,20 +73,50 @@
     X,
     Z,
     T,
-    own,
+    pipe_in,
+    doc_lengths,
+    norm_in,
+    w_query,
+    w_key,
+    w_value,
+    w_out_gate,
+    w_rank_down,
+    w_rank_up,
+    rank_bias,
+    head_gain,
+    w_out,
+    norm_mid,
+    w_gate,
+    w_up,
+    w_down,
+    ends,
+    g_norm_in,
+    g_query,
+    g_key,
+    g_value,
+    g_out_gate,
+    g_rank_down,
+    g_rank_up,
+    g_rank_bias,
+    g_head_gain,
+    g_out,
+    g_norm_mid,
+    g_gate,
+    g_up,
+    g_down,
+    W,
     shard,
-    norm_in,
-    norm_mid,
+    tiles,
+    line,
+    pick_gain,
+    pick_bias,
+    pick_up,
+    rows_of,
     gain,
     bias,
-    rank_down,
     rank_up,
     allowed,
     aux,
-    ends,
-    og,
-    sg,
-    W,
     xbuf,
     x1,
     normed,
@@ -111,8 +144,17 @@
     GC,
     Q,
     RF,
+    og,
     dqkvg,
     dmix,
+    small_rows,
+    EG,
+    EY,
+    EB,
+    ES,
+    EO,
+    EX,
+    EZ,
     a_sem,
     gs,
     gr,
@@ -121,14 +163,22 @@
     ss,
     sr,
     e_sem,
+    t_sem,
+    u_sem,
+    v_sem,
 ):
     c = lax.axis_index("section")
     d = lax.axis_index("dp")
     t = lax.axis_index("tensor")
     x, z = d // Z, d % Z
     o = 1 - c
-    D = own.shape[-1]
-    R = shard.shape[0]
+    own = pipe_in.at[0]
+    D = pipe_in.shape[-1]
+    R = w_query.shape[1]
+    B = R // T
+    N = X * Z
+    G_RANK = w_rank_down.shape[2]
+    n_gain, n_bias = head_gain.shape[1], rank_bias.shape[1]
     H = R // 2
     TL = TOK // T
     size = (X, Z)
@@ -154,17 +204,90 @@
     pl.semaphore_signal(barrier, inc=1, device_id={"section": o}, device_id_type=MESH)
     pl.semaphore_wait(barrier, X + Z + T - 2)
 
+    def lanes(shape):
+        return lax.broadcasted_iota(jnp.int32, shape, len(shape) - 1)
+
+    def downs(shape):
+        return lax.broadcasted_iota(jnp.int32, shape, len(shape) - 2)
+
+    def column(ref, n):
+        line[...] = jnp.zeros_like(line)
+        line[0:1, 0:n] = wide(ref[...])
+        spread = jnp.broadcast_to(line[0:1, :], (B, 128))
+        return jnp.sum(jnp.where(lanes((B, 128)) == downs((B, 128)), spread, 0.0), axis=1, keepdims=True)
+
+    line[...] = jnp.zeros_like(line)
+    line[0:B, 0:G_RANK] = wide(w_rank_down[0])
+    tile = line[0:B, :]
+    lane, down = lanes((B, 128)), downs((B, 128))
+    for at, ref, n in (
+        (AT_IN, norm_in, B),
+        (AT_MID, norm_mid, B),
+        (AT_GAIN, head_gain, n_gain),
+        (AT_BIAS, rank_bias, n_bias),
+    ):
+        tile = jnp.where(lane == at, column(ref, n), tile)
+    second = wide(w_rank_up[0])
+    turned = pltpu.roll(jnp.broadcast_to(second, (8, 128)), 64, 1)[0:1]
+    tile = jnp.where(jnp.logical_and(down == 0, lane >= 64), turned, tile)
+    tile = jnp.where(jnp.logical_and(down == 1, lane >= 64), second, tile)
+    tiles[t] = low(tile)
+
+    def tile_copy(k):
+        s, r = t_sem.at[0, k - 1], t_sem.at[1, k - 1]
+        peer, source = (t + k) % T, (t - k) % T
+        return remote(tiles.at[t], tiles.at[t], s, r, tensor=peer), remote(
+            tiles.at[source], tiles.at[source], s, r, tensor=peer
+        )
+
+    for k in range(1, T):
+        tile_copy(k)[0].start()
+
+    MAIN = SMALL[0]
+    shard[:, 0:128] = w_query[0]
+    shard[:, 128:256] = w_key[0]
+    shard[:, 256:512] = w_value[0]
+    shard[:, 512:768] = w_out_gate[0]
+    shard[:, 768:1024] = low(wide(w_out[0]).T)
+    shard[:, GU[0] : GU[0] + FFM] = w_gate[0, :, :FFM]
+    shard[:, GU[0] + FFM : GU[0] + 2 * FFM] = w_up[0, :, :FFM]
+    shard[:, GU[0] + 2 * FFM : GU[0] + GU[1]] = jnp.concatenate(
+        [w_gate[0, :, FFM:], w_up[0, :, FFM:]], axis=1
+    )
+    shard[:, MAIN - 128 : MAIN] = jnp.zeros((R, 128), bf16)
+    shard[:, DOWN[0] : DOWN[0] + FFD] = low(wide(w_down[0]).T)
+
     half = lambda h: pl.ds(pl.multiple_of(h * H, H), H)
-    swap_w = remote(shard.at[half(o)], W.at[c, x, z, o], a_sem.at[0], a_sem.at[1], section=o)
+    main = pl.ds(0, MAIN)
+    extra = pl.ds(MAIN, SMALL[1])
+    swap_w = remote(
+        shard.at[half(o), main], W.at[c, x, z, o, :, main], a_sem.at[0], a_sem.at[1], section=o
+    )
     swap_x = remote(own.at[o], xbuf.at[c], a_sem.at[2], a_sem.at[3], section=o)
-    keep_w = pltpu.make_async_copy(shard.at[half(c)], W.at[c, x, z, c], a_sem.at[4])
+    keep_w = pltpu.make_async_copy(shard.at[half(c), main], W.at[c, x, z, c, :, main], a_sem.at[4])
     keep_x = pltpu.make_async_copy(own.at[c], xbuf.at[c], a_sem.at[5])
     swap_w.start()
     swap_x.start()
     keep_w.start()
     keep_x.start()
-    got_w = remote(shard.at[half(o)], W.at[o, x, z, c], a_sem.at[0], a_sem.at[1], section=o)
+    got_w = remote(
+        shard.at[half(o), main], W.at[o, x, z, c, :, main], a_sem.at[0], a_sem.at[1], section=o
+    )
     got_x = remote(own.at[o], xbuf.at[o], a_sem.at[2], a_sem.at[3], section=o)
+    swap_e = remote(
+        shard.at[half(o), extra], W.at[c, x, z, o, :, extra], a_sem.at[6], a_sem.at[7], section=o
+    )
+    got_e = remote(
+        shard.at[half(o), extra], W.at[o, x, z, c, :, extra], a_sem.at[6], a_sem.at[7], section=o
+    )
+    keep_e = pltpu.make_async_copy(shard.at[half(c), extra], W.at[c, x, z, c, :, extra], a_sem.at[8])
+
+    def small_swap():
+        for k in range(1, T):
+            tile_copy(k)[1].wait_recv()
+        shard[:, MAIN:WIDE] = tiles[...].reshape(R, 128)
+        swap_e.start()
+        keep_e.start()
 
     def w_first(l, j, k):
         c0, n, axis = GATHER[j]
@@ -221,6 +344,50 @@
                 arrived.add((l, j))
                 w_third(l, j)[1].wait_recv()
         return W[l, :, :, :, :, c0 : c0 + n].reshape(D, n)
+
+    def prepare():
+        r, g = downs((D, HV)), lanes((D, HV))
+        pick_gain[...] = low(
+            jnp.where(jnp.logical_and(r % B < n_gain, r // B * n_gain + r % B == g), 1.0, 0.0)
+        )
+        r, g = downs((D, HK)), lanes((D, HK)) + t * HK
+        pick_bias[...] = low(
+            jnp.where(jnp.logical_and(r % B < n_bias, r // B * n_bias + r % B == g), 1.0, 0.0)
+        )
+        r, g = downs((128, D)), lanes((128, D))
+        for i in range(2):
+            pick_up[i] = low(jnp.where(g == r * R + t * B + i, 1.0, 0.0))
+        bounds, total = [], 0
+        for j in range(doc_lengths.shape[1]):
+            total = total + doc_lengths[c, j]
+            bounds.append(total)
+
+        def segment(at):
+            seg = jnp.zeros(at.shape, jnp.int32)
+            for bound in bounds:
+                seg = seg + jnp.where(bound <= at, 1, 0)
+            return seg
+
+        i, j = downs((TOK, TOK)), lanes((TOK, TOK))
+        same = jnp.logical_and(i // CH == j // CH, segment(i) == segment(j))
+        allowed[...] = jnp.where(jnp.logical_and(i >= j, same), 1.0, 0.0)
+        i, lane = downs((TOK, 128)), lanes((TOK, 128))
+        first = i // CH * CH
+        seg, before, last = segment(i), segment(first - 1), segment(first + CH - 1)
+        one = lambda v: jnp.where(v, 1.0, 0.0)
+        aux[...] = jnp.where(
+            lane == 0, one(seg == before), jnp.where(lane == 1, one(seg == last), one(last == before))
+        )
+
+    def small_whole(l):
+        every = weight(l, SMALL)
+        pick = low(jnp.where(lanes((16, 128)) == downs((16, 128)) + AT_IN, 1.0, 0.0))
+        found = dot_back(pick, every)
+        rows_of[l] = found
+        gain[l] = dot(low(found), pick_gain[...])[2:3]
+        bias[l] = dot(low(found), pick_bias[...])[3:4]
+        first, second = dot(pick_up[0], every), dot(pick_up[1], every)
+        rank_up[l] = low(jnp.where(lanes((128, 128)) < 64, pltpu.roll(first, 64, 1), second))
 
     def rows(p):
         return pl.ds(pl.multiple_of(p * TL, TL), TL)
@@ -363,12 +530,13 @@
         return dot(tri, first) + (dot(tri, second) + dot(tri, third))
 
     def forward(l, i, x_ref, out_ref, hooks):
+        hooks[0]()
+        small_whole(l)
         xin = wide(x_ref[...])
-        normed[l] = low(xin * rms_scale(xin) * norm_in[l])
-        hooks[0]()
+        normed[l] = low(xin * rms_scale(xin) * rows_of[l, 0:1])
         nrm = normed[l]
         qkvg[l] = dot(nrm, weight(l, QKVG))
-        rank[l] = low(dot(nrm, rank_down[l]))
+        rank[l] = low(dot(nrm, weight(l, SMALL)))
         pre = dot(rank[l], rank_up[l]) + bias[l]
         soft = jnp.log1p(jnp.exp(-jnp.abs(pre)))
         slope[l] = jax.nn.sigmoid(-pre) / 16.0
@@ -378,11 +546,11 @@
         g = qkvg[l, :, 512:768]
         head = lax.rsqrt(jnp.mean(at * at, axis=-1, keepdims=True) + head_floor)
         mixed[l] = low(at * head * gain[l] * g * jax.nn.sigmoid(g))
+        hooks[1]()
         sum_start(i, dot_back(mixed[l], weight(l, OUT)))
-        hooks[1]()
         hidden = wide(x_ref[rows(t)]) + sum_wait(i)
         hid[l] = hidden
-        share_start(i + 1, nm.at[l], hidden * rms_scale(hidden) * norm_mid[l])
+        share_start(i + 1, nm.at[l], hidden * rms_scale(hidden) * rows_of[l, 1:2])
         hooks[2]()
         w_gu = weight(l, GU)
         share_wait(i + 1, nm.at[l])
@@ -472,6 +640,83 @@
         d_decay = running(jnp.concatenate(out_b, axis=0), True)
         return low(d_decay * slope[l]), d_gain
 
+    def small_copy(l, k):
+        peer = (t + k) % T
+        return remote(
+            EG.at[l, :, :, peer], EB.at[l, k - 1], u_sem.at[l, 0, k - 1], u_sem.at[l, 1, k - 1], tensor=peer
+        )
+
+    def small_gradients(l, d_rank, d_pre, d_gain):
+        rank_rows = downs((16, HV))
+        at_gain = low(jnp.where(rank_rows == 2, d_gain, 0.0))
+        d_bias = jnp.sum(wide(d_pre), axis=0, keepdims=True)
+        at_bias = low(jnp.where(downs((16, HK)) == 3, d_bias, 0.0))
+        found = small_rows[l] + dot_back(at_gain, pick_gain[...]) + dot_back(at_bias, pick_bias[...])
+        pick = low(jnp.where(lanes((16, 128)) == downs((16, 128)) + AT_IN, 1.0, 0.0))
+        ups = dot_grad(rank[l], d_pre)
+        right = lanes((128, 128)) >= 64
+        every = (
+            dot_grad(normed[l], d_rank)
+            + dot_grad(low(found), pick)
+            + dot_grad(pick_up[0], low(jnp.where(right, pltpu.roll(ups, 64, 1), 0.0)))
+            + dot_grad(pick_up[1], low(jnp.where(right, ups, 0.0)))
+        )
+        EG[l] = low(every).reshape(X, Z, T, B, 128)
+        for k in range(1, T):
+            small_copy(l, k).start()
+
+    def small_sum(l):
+        total = wide(EG[l, :, :, t])
+        for k in range(1, T):
+            small_copy(l, k).wait()
+            total = total + wide(EB[l, k - 1])
+        EY[l] = low(total)
+
+    small_swap_out = remote(EY.at[o], EO, v_sem.at[0, 0], v_sem.at[0, 1], section=o)
+
+    def small_x(k):
+        return remote(
+            ES.at[(x + k) % X], EX.at[k - 1], v_sem.at[k, 0], v_sem.at[k, 1], dp=dp_peer(0, k)
+        )
+
+    def small_z(k):
+        return remote(
+            ES.at[x, (z + k) % Z], EZ.at[k - 1], v_sem.at[3 + k, 0], v_sem.at[3 + k, 1], dp=dp_peer(1, k)
+        )
+
+    def small_first():
+        small_swap_out.wait()
+        ES[...] = low(wide(EY[c]) + wide(EO[...]))
+        for k in range(1, X):
+            small_x(k).start()
+
+    def small_second():
+        total = wide(ES[x])
+        for k in range(1, X):
+            small_x(k).wait()
+            total = total + wide(EX[k - 1])
+        ES[x] = low(total)
+        for k in range(1, Z):
+            small_z(k).start()
+
+    def small_third():
+        total = wide(ES[x, z])
+        for k in range(1, Z):
+            small_z(k).wait()
+            total = total + wide(EZ[k - 1])
+        g_rank_down[0] = total[:, 0:G_RANK]
+        turn = lanes((B, 128)) == downs((B, 128))
+        for at, ref, n in (
+            (AT_IN, g_norm_in, B),
+            (AT_MID, g_norm_mid, B),
+            (AT_GAIN, g_head_gain, n_gain),
+            (AT_BIAS, g_rank_bias, n_bias),
+        ):
+            row = jnp.sum(jnp.where(turn, total[:, at : at + 1], 0.0), axis=0, keepdims=True)
+            ref[...] = row[:, 0:n]
+        turned = pltpu.roll(total[0:8], 64, 1)[0:1]
+        g_rank_up[0] = jnp.where(lanes((1, 128)) < 64, turned, total[1:2])
+
     def backward(l, i, x_ref, dy_ref, out_ref, hooks):
         dy = dy_ref[...]
         d_inner = dot(dy, weight(l, DOWN))
@@ -493,55 +738,62 @@
         hidden = hid[l]
         scale_mid = rms_scale(hidden)
         unit = hidden * scale_mid
-        sg[l, 17:18, :] = jnp.sum(d_mid * unit, axis=0, keepdims=True)
-        scaled = d_mid * norm_mid[l]
+        small_rows[l] = jnp.zeros((16, D), f32)
+        small_rows[l, 1:2] = jnp.sum(d_mid * unit, axis=0, keepdims=True)
+        scaled = d_mid * rows_of[l, 1:2]
         d_hidden = wide(dy_ref[rows(t)]) + scale_mid * (
             scaled - unit * jnp.mean(scaled * unit, axis=-1, keepdims=True)
         )
         hid[l] = d_hidden
-        share_start(i + 1, dh.at[l], d_hidden)
+        share_start(i + 1, dh, d_hidden)
         hooks[1]()
-        share_wait(i + 1, dh.at[l])
-        dmix[...] = dot(dh[l], weight(l, OUT))
+        share_wait(i + 1, dh)
+        dmix[...] = dot(dh[...], weight(l, OUT))
         d_pre, d_gain = mixer_backward(l)
         d_rank = low(dot_back(d_pre, rank_up[l]))
-        sum_start(i + 2, dot_back(dqkvg[...], weight(l, QKVG)) + dot_back(d_rank, rank_down[l]))
+        partial = dot_back(dqkvg[...], weight(l, QKVG)) + dot_back(d_rank, weight(l, SMALL))
+        sum_start(i + 2, partial)
+        xin = wide(x_ref[...])
+        small_rows[l, 0:1] = jnp.sum(partial * (xin * rms_scale(xin)), axis=0, keepdims=True)
         hooks[2]()
-        put(OUT, dh[l], mixed[l])
+        put(OUT, dh[...], mixed[l])
         scatter_swap(l, 2)
         put(QKVG, normed[l], dqkvg[...])
         scatter_swap(l, 3)
         scatter_swap(l, 4)
-        sg[l, 0:16, :] = dot_grad(d_rank, normed[l])[0:16]
-        sg[l, 18:19, 0:HV] = d_gain
-        sg[l, 19:20, 0:HK] = jnp.sum(wide(d_pre), axis=0, keepdims=True)
-        sg[l, 24:40, 0:HK] = dot_grad(rank[l], d_pre)[0:16]
+        small_gradients(l, d_rank, d_pre, d_gain)
         hooks[3]()
         d_normed = sum_wait(i + 2)
         xin = wide(x_ref[rows(t)])
         scale_in = rms_scale(xin)
         unit = xin * scale_in
-        sg[l, 16:17, :] = jnp.sum(d_normed * unit, axis=0, keepdims=True)
-        scaled = d_normed * norm_in[l]
+        scaled = d_normed * rows_of[l, 0:1]
         dx = hid[l] + scale_in * (scaled - unit * jnp.mean(scaled * unit, axis=-1, keepdims=True))
         share_start(i + 3, out_ref, dx)
 
     def nothing():
         pass
 
-    count = len(GATHER)
+    early, late = (6, 0, 1), (2, 3, 4, 5)
 
     def first_weights():
+        prepare()
+        small_swap()
         got_w.wait_recv()
         keep_w.wait()
-        for j in range(count):
+        for j in early[1:]:
             gather_first(0, j)
-        for j in range(count):
+        got_e.wait_recv()
+        keep_e.wait()
+        gather_first(0, early[0])
+        for j in early:
             gather_second(0, j)
-        for j in range(count):
+        for j in late:
+            gather_first(0, j)
+        for j in early:
             gather_third(0, j)
-        for j in range(count):
-            gather_first(1, j)
+        for j in late:
+            gather_second(0, j)
 
     def each(step, l, which):
         def run():
@@ -550,17 +802,22 @@
 
         return run
 
-    sg[...] = jnp.zeros_like(sg)
     got_x.wait_recv()
     keep_x.wait()
-    everything = range(count)
+    everything = early + late
     forward(
         0,
         0,
         xbuf.at[0],
         x1,
-        (first_weights, each(gather_second, 1, everything), nothing, each(gather_third, 1, everything)),
-    )
+        (
+            first_weights,
+            each(gather_third, 0, late),
+            each(gather_first, 1, everything),
+            each(gather_second, 1, everything),
+        ),
+    )
+    each(gather_third, 1, everything)()
     share_wait(3, x1)
     forward(1, 4, x1, res.at[1], (nothing, nothing, nothing, nothing))
 
@@ -587,6 +844,7 @@
     def in_second():
         each(scatter_first, 0, ff)()
         each(scatter_third, 1, mix)()
+        small_sum(1)
 
     backward(
         0,
@@ -597,23 +855,43 @@
         (each(scatter_second, 1, mix), in_second, each(scatter_second, 0, ff), each(scatter_third, 0, ff)),
     )
     each(scatter_first, 0, mix)()
+    small_sum(0)
+    small_swap_out.start()
     share_wait(15, res.at[0])
     give_end = remote(res.at[o], res_in, e_sem.at[0], e_sem.at[1], section=o)
     give_end.start()
+    small_first()
     each(scatter_second, 0, mix)()
-    ends[c] = wide(res[c])
+    small_second()
+    ends[0, c] = wide(res[c])
     each(scatter_third, 0, mix)()
     give_grad = remote(RF.at[o], og.at[c], e_sem.at[2], e_sem.at[3], section=o)
     got_grad = remote(RF.at[o], og.at[o], e_sem.at[2], e_sem.at[3], section=o)
     give_grad.start()
     og[c] = RF[c]
     give_end.wait_recv()
-    ends[o] = wide(res_in[...])
+    ends[0, o] = wide(res_in[...])
+    small_third()
     got_grad.wait_recv()
+    whole = lambda c0, n: og[:, :, c0 : c0 + n].reshape(R, n)
+    g_query[0] = whole(0, 128)
+    g_key[0] = whole(128, 128)
+    g_value[0] = whole(256, 256)
+    g_out_gate[0] = whole(512, 256)
+    g_out[0] = whole(*OUT).T
+    g_gate[0, :, :FFM] = whole(GU[0], FFM)
+    g_up[0, :, :FFM] = whole(GU[0] + FFM, FFM)
+    both = whole(GU[0] + 2 * FFM, 128)
+    g_gate[0, :, FFM:] = both[:, 0:64]
+    g_up[0, :, FFM:] = pltpu.roll(both, 64, 1)[:, 0:64]
+    g_down[0] = whole(*DOWN).T[0:FFD]
     give_end.wait_send()
     give_grad.wait_send()
     swap_w.wait_send()
     swap_x.wait_send()
+    swap_e.wait_send()
+    for k in range(1, T):
+        tile_copy(k)[0].wait_send()
     for l in range(2):
         for j, (_, _, axis) in enumerate(GATHER):
             for k in range(1, size[axis]):
@@ -623,12 +901,26 @@
             w_third(l, j)[0].wait_send()
 
 
-def run_kernel(X, Z, T, D, R, operands):
-    H = R // 2
-    TL = TOK // T
+def on_device(X, Z, *operands):
+    T = lax.axis_size("tensor")
+    D = operands[0].shape[-1]
+    R = operands[3].shape[1]
+    H, TL, B, N = R // 2, TOK // T, R // T, X * Z
     top = max(X, Z)
     scratch = [
         pltpu.VMEM((2, X, Z, 2, H, WIDE), bf16),
+        pltpu.VMEM((R, WIDE), bf16),
+        pltpu.VMEM((T, B, 128), bf16),
+        pltpu.VMEM((max(B, 8), 128), f32),
+        pltpu.VMEM((D, HV), bf16),
+        pltpu.VMEM((D, HK), bf16),
+        pltpu.VMEM((2, 128, D), bf16),
+        pltpu.VMEM((2, 16, D), f32),
+        pltpu.VMEM((2, 1, HV), f32),
+        pltpu.VMEM((2, 1, HK), f32),
+        pltpu.VMEM((2, 128, HK), bf16),
+        pltpu.VMEM((TOK, TOK), f32),
+        pltpu.VMEM((TOK, 128), f32),
         pltpu.VMEM((2, TOK, D), bf16),
         pltpu.VMEM((TOK, D), bf16),
         pltpu.VMEM((2, TOK, D), bf16),
@@ -644,21 +936,30 @@
         pltpu.VMEM((2, TOK, GU[1]), f32),
         pltpu.VMEM((2, TOK, DOWN[1]), bf16),
         pltpu.VMEM((2, TOK, 128), bf16),
-        pltpu.VMEM((2, TOK, D), bf16),
+        pltpu.VMEM((TOK, D), bf16),
         pltpu.VMEM((TOK, D), bf16),
         pltpu.VMEM((2, TOK, D), bf16),
         pltpu.VMEM((TOK, D), bf16),
         pltpu.VMEM((2, TOK, D), bf16),
         pltpu.VMEM((2, T - 1, TL, D), bf16),
-        pltpu.VMEM((X, Z, 2, H, WIDE), bf16),
-        pltpu.VMEM((2, X, Z, H, WIDE), bf16),
-        pltpu.VMEM((2, top - 1, top, H, WIDE), bf16),
-        pltpu.VMEM((2, top - 1, H, WIDE), bf16),
-        pltpu.VMEM((2, top, H, WIDE), bf16),
-        pltpu.VMEM((2, H, WIDE), f32),
+        pltpu.VMEM((X, Z, 2, H, SMALL[0]), bf16),
+        pltpu.VMEM((2, X, Z, H, SMALL[0]), bf16),
+        pltpu.VMEM((2, top - 1, top, H, SMALL[0]), bf16),
+        pltpu.VMEM((2, top - 1, H, SMALL[0]), bf16),
+        pltpu.VMEM((2, top, H, SMALL[0]), bf16),
+        pltpu.VMEM((2, H, SMALL[0]), f32),
+        pltpu.VMEM((2, H, SMALL[0]), f32),
         pltpu.VMEM((TOK, 768), bf16),
         pltpu.VMEM((TOK, HV), f32),
-        pltpu.SemaphoreType.DMA((6,)),
+        pltpu.VMEM((2, 16, D), f32),
+        pltpu.VMEM((2, X, Z, T, B, 128), bf16),
+        pltpu.VMEM((2, X, Z, B, 128), bf16),
+        pltpu.VMEM((2, T - 1, X, Z, B, 128), bf16),
+        pltpu.VMEM((X, Z, B, 128), bf16),
+        pltpu.VMEM((X, Z, B, 128), bf16),
+        pltpu.VMEM((X - 1, Z, B, 128), bf16),
+        pltpu.VMEM((Z - 1, B, 128), bf16),
+        pltpu.SemaphoreType.DMA((9,)),
         pltpu.SemaphoreType.DMA((2, len(GATHER), 7)),
         pltpu.SemaphoreType.DMA((2, len(GATHER), 7)),
         pltpu.SemaphoreType.DMA((16, T - 1)),
@@ -666,147 +967,26 @@
         pltpu.SemaphoreType.DMA((2, len(SCATTER), 7)),
         pltpu.SemaphoreType.DMA((2, len(SCATTER), 7)),
         pltpu.SemaphoreType.DMA((4,)),
+        pltpu.SemaphoreType.DMA((2, T - 1)),
+        pltpu.SemaphoreType.DMA((2, 2, T - 1)),
+        pltpu.SemaphoreType.DMA((7, 2)),
     ]
+    order = (2, 3, 4, 5, 6, 7, 8, 9, 10, 11, 12, 13, 14, 15)
+    outs = (jax.ShapeDtypeStruct((1, 2, TOK, D), f32),) + tuple(
+        jax.ShapeDtypeStruct(operands[k].shape, f32) for k in order
+    )
     vmem = pl.BlockSpec(memory_space=pltpu.VMEM)
+    smem = pl.BlockSpec(memory_space=pltpu.SMEM)
     return pl.pallas_call(
         functools.partial(kernel, X, Z, T),
-        out_shape=(
-            jax.ShapeDtypeStruct((2, TOK, D), f32),
-            jax.ShapeDtypeStruct((2, H, WIDE), f32),
-            jax.ShapeDtypeStruct((2, 40, D), f32),
-        ),
-        in_specs=[vmem] * len(operands),
-        out_specs=(vmem,) * 3,
+        out_shape=outs,
+        in_specs=[vmem, smem] + [vmem] * (len(operands) - 2),
+        out_specs=(vmem,) * len(outs),
         scratch_shapes=scratch,
         compiler_params=pltpu.CompilerParams(
-            collective_id=0, has_side_effects=True, vmem_limit_bytes=63 * 1024 * 1024
+            collective_id=0, has_side_effects=True, vmem_limit_bytes=64 * 1024 * 1024 - 65536
         ),
     )(*operands)
-
-
-def mask_arrays(lengths):
-    bounds = jnp.cumsum(lengths)
-    places = jnp.arange(TOK, dtype=jnp.int32)
-    seg = jnp.sum((bounds[None, :] <= places[:, None]).astype(jnp.int32), axis=1)
-    by_block = seg.reshape(BLOCKS, CH)
-    last = by_block[:, CH - 1]
-    before = jnp.concatenate([jnp.full((1,), -1, jnp.int32), last[:-1]])
-    carried = (by_block == before[:, None]).reshape(TOK).astype(f32)
-    tail = (by_block == last[:, None]).reshape(TOK).astype(f32)
-    retain = jnp.broadcast_to((last == before)[:, None], (BLOCKS, CH)).reshape(TOK).astype(f32)
-    block = places // CH
-    allowed = (
-        (places[:, None] >= places[None, :])
-        & (block[:, None] == block[None, :])
-        & (seg[:, None] == seg[None, :])
-    ).astype(f32)
-    aux = jnp.pad(jnp.stack([carried, tail, retain], axis=1), ((0, 0), (0, 125)))
-    return allowed, aux
-
-
-def on_device(
-    X,
-    Z,
-    pipe_in,
-    doc_lengths,
-    norm_in,
-    w_query,
-    w_key,
-    w_value,
-    w_out_gate,
-    w_rank_down,
-    w_rank_up,
-    rank_bias,
-    head_gain,
-    w_out,
-    norm_mid,
-    w_gate,
-    w_up,
-    w_down,
-):
-    T = lax.axis_size("tensor")
-    N = X * Z
-    c = lax.axis_index("section")
-    d = lax.axis_index("dp")
-    t = lax.axis_index("tensor")
-    R = w_query.shape[1]
-    D = R * N
-    shard = jnp.concatenate(
-        [
-            w_query[0],
-            w_key[0],
-            w_value[0],
-            w_out_gate[0],
-            w_out[0].T,
-            w_gate[0, :, :FFM],
-            w_up[0, :, :FFM],
-            w_gate[0, :, FFM:],
-            w_up[0, :, FFM:],
-            w_down[0].T,
-            jnp.zeros((R, 2 * FFM + 128 - 2 * FFD + DOWN[1] - FFD), bf16),
-        ],
-        axis=1,
-    )
-    mine = [norm_in[0], norm_mid[0], head_gain[0], rank_bias[0], w_rank_down[0].reshape(-1), w_rank_up[0, 0]]
-    widths = [a.shape[0] for a in mine]
-    smalls = lax.all_gather(jnp.concatenate(mine), ("section", "dp", "tensor"), axis=0, tiled=False)
-    smalls = smalls.reshape(2, N, T, -1)
-    parts, at = [], 0
-    for w in widths:
-        parts.append(smalls[..., at : at + w])
-        at += w
-    g_in = parts[0].reshape(2, 1, D).astype(f32)
-    g_mid = parts[1].reshape(2, 1, D).astype(f32)
-    g_head = parts[2].reshape(2, 1, HV).astype(f32)
-    bias = lax.dynamic_slice_in_dim(parts[3].reshape(2, 1, T * HK).astype(f32), t * HK, HK, 2)
-    G = w_rank_down.shape[2]
-    down = jnp.pad(parts[4].reshape(2, D, G), ((0, 0), (0, 0), (0, 128 - G)))
-    up = lax.dynamic_index_in_dim(parts[5], t, 2, keepdims=False)
-    up = jnp.pad(up, ((0, 0), (0, 128 - N), (0, 0)))
-    allowed, aux = mask_arrays(lax.dynamic_index_in_dim(doc_lengths, c, 0, keepdims=False))
-    operands = (pipe_in[0], shard, g_in, g_mid, g_head, bias, down, up, allowed, aux)
-    ends, og, sg = run_kernel(X, Z, T, D, R, operands)
-    og = og.reshape(R, WIDE)
-    head = jnp.zeros((2, 1, T * HK), f32)
-    head = lax.dynamic_update_slice_in_dim(head, sg[:, 19:20, 0:HK], t * HK, 2)
-    ups = jnp.zeros((2, T, N * HK), f32)
-    ups = lax.dynamic_update_slice_in_dim(ups, sg[:, 24 : 24 + N, 0:HK].reshape(2, 1, N * HK), t, 1)
-    flat = jnp.concatenate(
-        [sg[:, 0:18].reshape(2, -1), sg[:, 18, 0:HV], head.reshape(2, -1), ups.reshape(2, -1)], axis=1
-    )
-    flat = lax.psum(flat, ("section", "dp", "tensor"))
-    flat = lax.dynamic_index_in_dim(flat, c, 0, keepdims=False)
-    place = d * T + t
-    block = D // (N * T)
-    table = flat[: 18 * D].reshape(18, D)
-    table = lax.dynamic_slice_in_dim(table, place * block, block, 1)
-    at = 18 * D
-    o_gain = lax.dynamic_slice_in_dim(flat[at : at + HV], place * (HV // (N * T)), HV // (N * T), 0)
-    at += HV
-    o_bias = lax.dynamic_slice_in_dim(
-        flat[at : at + T * HK], place * (T * HK // (N * T)), T * HK // (N * T), 0
-    )
-    at += T * HK
-    o_up = lax.dynamic_index_in_dim(flat[at:].reshape(T, N, HK), t, 0, keepdims=False)
-    o_up = lax.dynamic_slice_in_dim(o_up, d, 1, 0)
-    gates = og[:, GU[0] : GU[0] + GU[1]]
-    return (
-        ends[None],
-        table[16][None],
-        og[None, :, 0:128],
-        og[None, :, 128:256],
-        og[None, :, 256:512],
-        og[None, :, 512:768],
-        table[0:G].T[None],
-        o_up[None],
-        o_bias[None],
-        o_gain[None],
-        og[:, OUT[0] : OUT[0] + OUT[1]].T[None],
-        table[17][None],
-        jnp.concatenate([gates[:, :FFM], gates[:, 2 * FFM : 2 * FFM + 64]], axis=1)[None],
-        jnp.concatenate([gates[:, FFM : 2 * FFM], gates[:, 2 * FFM + 64 :]], axis=1)[None],
-        og[:, DOWN[0] : DOWN[0] + FFD].T[None],
-    )
 
 
 def solution(mesh):

time: 517 us -> 223 us (0.43)
  waiting for transfers between devices: 274 us -> 0 us
  local copies, waits for them, and re-layouts: 34.4 us -> 16.9 us
  Pallas kernels: 189 us -> 205 us
  between operations: 14.3 us -> 0.74 us
    psum x1 -> x0, waiting for transfers between devices: 137 us -> none  [on_device(): flat = lax.psum(flat, ('section', 'dp', 'tensor'))]
    unnamed x3 -> x0, waiting for transfers between devices: 137 us -> none
    pallas_call x1, Pallas kernels: 189 us -> 205 us  [on_device(): pl.pallas_call(functools.partial(kernel, X, Z, T), out_shape=outs, in_spe...]
    unnamed x15 -> x39, local copies, waits for them, and re-layouts: 4.03 us -> 13.5 us
    slice x13 -> x0, local copies, waits for them, and re-layouts: 7.38 us -> none  [the longest x1 1.12 us: on_device(): table = flat[:18 * D].reshape(18, D)]
    concatenate x2 -> x0, local copies, waits for them, and re-layouts: 5.27 us -> none  [the longest x1 3.43 us: on_device(): jnp.concatenate(mine)]
  transfers between devices with their start and end apart: 2 -> 0, of which waited for: 2 -> 0; matrix products, arithmetic and copies ran while one was open for 2% -> 0% of each run, Pallas kernels for 0% -> 0%
where the time goes in v1:
time: 223 us
  Pallas kernels  205 us (92%)
  local copies, waits for them, and re-layouts  16.9 us (8%)
    pallas_call x1, Pallas kernels, on_device(): pl.pallas_call(functools.partial(kernel, X, Z, T), out_shape=outs, in_spe...  205 us
    unnamed x39, local copies, waits for them, and re-layouts  13.5 us

profile of v1, /device:TPU:1, one launch (start us, length us, event | category | flops | bytes accessed | tf_op | source)
XLA Modules:
  0.0 222.6 jit_solution(3767626829190814065)
XLA Ops:
  0.6 1.5 copy.31.w_out
  2.1 1.7 copy.32.w_down
  3.8 204.9 %shard_map.271 = (f32[1,2,256,1024]{3,2,1,0:T(8,128)}, f32[1,16]{1,0:T(1,128)}, f32[1,64,128]{2,1,0:T(8,128)}, f32[1,64,128]{2,1,0:T(8,128)}, f32[1,64,256]{2,1,...) custom-call(bf16[1,2,256,1024]{3,2,1,0:T(8,128)(2,1)} %pipe_in.1, ...), custom_call_target="tpu_custom_call" | custom-call | tf_op jit(solution)/shard_map/pallas_call | solution.py:980
  208.8 1.6 copy.33
  210.4 1.8 copy.34
  212.2 0.0 copy-start.11
  212.2 0.0 copy-start.5
  212.2 0.0 copy-start.4
  212.2 0.0 copy-start.3
  212.2 0.0 copy-start.2
  212.2 0.0 copy-start.6
  212.2 0.0 copy-start.10
  212.2 0.0 copy-start.9
  212.2 0.0 copy-start.8
  212.3 0.0 copy-start.7
  212.3 0.0 copy-start.1
  212.3 0.0 copy-start
  212.3 3.2 %copy.48 = f32[1,2,256,1024]{3,2,1,0:T(8,128)} copy(f32[1,2,256,1024]{3,2,1,0:T(8,128)} %get-tuple-element.45) | data formatting | bytes 4194304
  215.5 0.0 copy-done.11
  215.5 0.5 copy.49
  216.0 0.0 copy-done.5
  216.0 0.6 copy.50
  216.7 0.0 copy-done.4
  216.7 0.6 copy.51
  217.3 0.0 copy-done.3
  217.3 0.6 copy.52
  217.9 0.0 copy-done.2
  217.9 0.6 copy.53
  218.5 0.0 copy-done.6
  218.5 0.6 copy.54
  219.1 0.0 copy-done.10
  219.1 0.5 copy.55
  219.7 0.0 copy-done.9
  219.7 0.5 copy.56
  220.2 0.0 copy-done.8
  220.2 0.5 copy.57
  220.7 0.0 copy-done.7
  220.7 0.5 copy.58
  221.2 0.0 copy-done.1
  221.2 0.7 copy.59
  221.9 0.0 copy-done
  221.9 0.7 copy.60
Async XLA Ops:
  212.2 3.3 %copy-start.11 = (f32[1,16]{1,0:T(1,128)S(1)}, f32[1,16]{1,0:T(1,128)}, u32[]{:S(2)}) copy-start(f32[1,16]{1,0:T(1,128)} %get-tuple-element.46) | copy-start | bytes 196
  212.2 3.9 %copy-start.5 = (f32[1,64,128]{2,1,0:T(8,128)S(1)}, f32[1,64,128]{2,1,0:T(8,128)}, u32[]{:S(2)}) copy-start(f32[1,64,128]{2,1,0:T(8,128)} %get-tuple-element.47) | copy-start | bytes 98308
  212.2 4.5 %copy-start.4 = (f32[1,64,128]{2,1,0:T(8,128)S(1)}, f32[1,64,128]{2,1,0:T(8,128)}, u32[]{:S(2)}) copy-start(f32[1,64,128]{2,1,0:T(8,128)} %get-tuple-element.48) | copy-start | bytes 98308
  212.2 5.1 %copy-start.3 = (f32[1,64,256]{2,1,0:T(8,128)S(1)}, f32[1,64,256]{2,1,0:T(8,128)}, u32[]{:S(2)}) copy-start(f32[1,64,256]{2,1,0:T(8,128)} %get-tuple-element.49) | copy-start | bytes 196612
  212.2 5.7 %copy-start.2 = (f32[1,64,256]{2,1,0:T(8,128)S(1)}, f32[1,64,256]{2,1,0:T(8,128)}, u32[]{:S(2)}) copy-start(f32[1,64,256]{2,1,0:T(8,128)} %get-tuple-element.50) | copy-start | bytes 196612
  212.2 6.3 %copy-start.6 = (f32[1,16,16]{2,1,0:T(8,128)S(1)}, f32[1,16,16]{2,1,0:T(8,128)}, u32[]{:S(2)}) copy-start(f32[1,16,16]{2,1,0:T(8,128)} %get-tuple-element.51) | copy-start | bytes 3076
  212.2 6.9 %copy-start.10 = (f32[1,1,128]{2,1,0:T(1,128)S(1)}, f32[1,1,128]{2,1,0:T(1,128)}, u32[]{:S(2)}) copy-start(f32[1,1,128]{2,1,0:T(1,128)} %get-tuple-element.52) | copy-start | bytes 1540
  212.2 7.4 %copy-start.9 = (f32[1,8]{1,0:T(1,128)S(1)}, f32[1,8]{1,0:T(1,128)}, u32[]{:S(2)}) copy-start(f32[1,8]{1,0:T(1,128)} %get-tuple-element.53) | copy-start | bytes 100
  212.2 7.9 %copy-start.8 = (f32[1,4]{1,0:T(1,128)S(1)}, f32[1,4]{1,0:T(1,128)}, u32[]{:S(2)}) copy-start(f32[1,4]{1,0:T(1,128)} %get-tuple-element.54) | copy-start | bytes 52
  212.3 8.4 %copy-start.7 = (f32[1,16]{1,0:T(1,128)S(1)}, f32[1,16]{1,0:T(1,128)}, u32[]{:S(2)}) copy-start(f32[1,16]{1,0:T(1,128)} %get-tuple-element.56) | copy-start | bytes 196
  212.3 8.9 %copy-start.1 = (f32[1,64,704]{2,1,0:T(8,128)S(1)}, f32[1,64,704]{2,1,0:T(8,128)}, u32[]{:S(2)}) copy-start(f32[1,64,704]{2,1,0:T(8,128)} %get-tuple-element.57) | copy-start | bytes 540676
  212.3 9.6 %copy-start = (f32[1,64,704]{2,1,0:T(8,128)S(1)}, f32[1,64,704]{2,1,0:T(8,128)}, u32[]{:S(2)}) copy-start(f32[1,64,704]{2,1,0:T(8,128)} %get-tuple-element.58) | copy-start | bytes 540676

commit v2 on v1

--- a/solution.py
+++ b/solution.py
@@ -30,11 +30,12 @@
 GATHER = (
     (0, 384, 0),
     (384, 384, 1),
-    (768, 768, 0),
-    (1536, 896, 1),
-    (2432, 384, 0),
-    (2816, 384, 1),
-    (3200, 128, 0),
+    (768, 256, 0),
+    (1024, 640, 1),
+    (1664, 768, 0),
+    (2432, 384, 1),
+    (2816, 384, 0),
+    (3200, 128, 1),
 )
 SCATTER = (
     (1024, 1408, 0),
@@ -129,13 +130,13 @@
     attn,
     mixed,
     hid,
+    d_hid,
     gu,
     inner,
     rank,
     dh,
     dy0,
     res,
-    res_in,
     pbuf,
     rbuf,
     G,
@@ -146,7 +147,10 @@
     RF,
     og,
     dqkvg,
-    dmix,
+    d_gu,
+    d_pre,
+    d_rank,
+    d_states,
     small_rows,
     EG,
     EY,
@@ -180,7 +184,8 @@
     G_RANK = w_rank_down.shape[2]
     n_gain, n_bias = head_gain.shape[1], rank_bias.shape[1]
     H = R // 2
-    TL = TOK // T
+    HALF = TOK // 2
+    S = HALF // T
     size = (X, Z)
     here = (x, z)
 
@@ -248,14 +253,14 @@
     shard[:, 128:256] = w_key[0]
     shard[:, 256:512] = w_value[0]
     shard[:, 512:768] = w_out_gate[0]
-    shard[:, 768:1024] = low(wide(w_out[0]).T)
+    shard[:, 768:1024] = w_out[0]
     shard[:, GU[0] : GU[0] + FFM] = w_gate[0, :, :FFM]
     shard[:, GU[0] + FFM : GU[0] + 2 * FFM] = w_up[0, :, :FFM]
     shard[:, GU[0] + 2 * FFM : GU[0] + GU[1]] = jnp.concatenate(
         [w_gate[0, :, FFM:], w_up[0, :, FFM:]], axis=1
     )
     shard[:, MAIN - 128 : MAIN] = jnp.zeros((R, 128), bf16)
-    shard[:, DOWN[0] : DOWN[0] + FFD] = low(wide(w_down[0]).T)
+    shard[:, DOWN[0] : DOWN[0] + FFD] = w_down[0]
 
     half = lambda h: pl.ds(pl.multiple_of(h * H, H), H)
     main = pl.ds(0, MAIN)
@@ -389,45 +394,49 @@
         first, second = dot(pick_up[0], every), dot(pick_up[1], every)
         rank_up[l] = low(jnp.where(lanes((128, 128)) < 64, pltpu.roll(first, 64, 1), second))
 
-    def rows(p):
-        return pl.ds(pl.multiple_of(p * TL, TL), TL)
-
-    def sum_copy(i, k):
+    def rows(p, h):
+        return pl.ds(pl.multiple_of(h * HALF + p * S, S), S)
+
+    def of(h):
+        return slice(h * HALF, (h + 1) * HALF)
+
+    def sum_copy(i, h, k):
         peer = (t + k) % T
+        into = rbuf.at[2 if i == 6 else i // 2 % 2, h, k - 1]
         return remote(
-            pbuf.at[i // 2 % 2, rows(peer)], rbuf.at[i // 2 % 2, k - 1], ys.at[i, k - 1], yr.at[i, k - 1], tensor=peer
-        )
-
-    def sum_start(i, part):
-        pbuf[i // 2 % 2] = low(part)
+            pbuf.at[i // 2 % 2, rows(peer, h)], into, ys.at[i, h, k - 1], yr.at[i, h, k - 1], tensor=peer
+        )
+
+    def sum_start(i, h, part):
+        pbuf[i // 2 % 2, of(h)] = low(part)
         for k in range(1, T):
-            sum_copy(i, k).start()
-
-    def sum_wait(i):
-        total = wide(pbuf[i // 2 % 2, rows(t)])
+            sum_copy(i, h, k).start()
+
+    def sum_wait(i, h):
+        total = wide(pbuf[i // 2 % 2, rows(t, h)])
         for k in range(1, T):
-            sum_copy(i, k).wait_recv()
-            total = total + wide(rbuf[i // 2 % 2, k - 1])
+            sum_copy(i, h, k).wait_recv()
+            total = total + wide(rbuf[2 if i == 6 else i // 2 % 2, h, k - 1])
         for k in range(1, T):
-            sum_copy(i, k).wait_send()
+            sum_copy(i, h, k).wait_send()
         return total
 
-    def share_copy(i, ref, k):
+    def share_copy(i, h, ref, k):
         peer = (t + k) % T
-        s, r = ys.at[i, k - 1], yr.at[i, k - 1]
-        mine, into = ref.at[rows(t)], ref.at[rows((t - k) % T)]
+        s, r = ys.at[i, h, k - 1], yr.at[i, h, k - 1]
+        mine, into = ref.at[rows(t, h)], ref.at[rows((t - k) % T, h)]
         return remote(mine, mine, s, r, tensor=peer), remote(into, into, s, r, tensor=peer)
 
-    def share_start(i, ref, value):
-        ref[rows(t)] = low(value)
+    def share_start(i, h, ref, value):
+        ref[rows(t, h)] = low(value)
         for k in range(1, T):
-            share_copy(i, ref, k)[0].start()
-
-    def share_wait(i, ref):
+            share_copy(i, h, ref, k)[0].start()
+
+    def share_wait(i, h, ref):
         for k in range(1, T):
-            share_copy(i, ref, k)[1].wait_recv()
+            share_copy(i, h, ref, k)[1].wait_recv()
         for k in range(1, T):
-            share_copy(i, ref, k)[0].wait_send()
+            share_copy(i, h, ref, k)[0].wait_send()
 
     def s_swap(l, j):
         c0, n, _ = SCATTER[j]
@@ -492,35 +501,37 @@
     scale = HK**-0.5
     sub = lambda v, n: v[n * CH : (n + 1) * CH]
 
-    def mixer_forward(l):
-        qk = qkvg[l]
-        b = cum[l]
+    def mixer_forward(l, h):
+        r = of(h)
+        qk = qkvg[l, r]
+        b = cum[l, r]
         qd = low(qk[:, 0:128] * scale * jnp.exp(b))
         kd = low(qk[:, 128:256] * jnp.exp(-b))
         v = low(qk[:, 256:512])
-        scores = low(jnp.where(allowed[...] > 0.0, dot_back(qd, kd), 0.0))
-        amat[l] = scores
+        scores = low(jnp.where(allowed[r, r] > 0.0, dot_back(qd, kd), 0.0))
+        amat[l, h] = scores
         within = dot(scores, v)
-        out = [sub(within, 0)]
-        state = None
-        for n in range(BLOCKS - 1):
-            bn = sub(b, n)
-            last = bn[CH - 1 : CH]
-            tail = sub(aux[...], n)[:, 1:2]
-            kt = low(sub(qk, n)[:, 128:256] * jnp.exp(last - bn) * tail)
-            fresh = dot_grad(sub(v, n), kt)
-            if state is None:
-                state = fresh
-            else:
-                state = aux[n * CH : n * CH + 1, 2:3] * jnp.exp(last) * state + fresh
-            states[l, n] = state
-            carried = sub(aux[...], n + 1)[:, 0:1]
-            out.append(sub(within, n + 1) + carried * dot_back(sub(qd, n + 1), low(state)))
-        attn[l] = jnp.concatenate(out, axis=0)
+        ax = aux[r]
+        out = []
+        for e in range(HALF // CH):
+            n = h * (HALF // CH) + e
+            here_out = sub(within, e)
+            if n > 0:
+                here_out = here_out + sub(ax, e)[:, 0:1] * dot_back(sub(qd, e), low(states[l, n - 1]))
+            out.append(here_out)
+            if n < BLOCKS - 1:
+                bn = sub(b, e)
+                last = bn[CH - 1 : CH]
+                kt = low(sub(qk, e)[:, 128:256] * jnp.exp(last - bn) * sub(ax, e)[:, 1:2])
+                state = dot_grad(sub(v, e), kt)
+                if n > 0:
+                    state = state + sub(ax, e)[0:1, 2:3] * jnp.exp(last) * states[l, n - 1]
+                states[l, n] = state
+        attn[l, r] = jnp.concatenate(out, axis=0)
 
     def running(v, upper):
-        row = lax.broadcasted_iota(jnp.int32, (TOK, TOK), 0)
-        col = lax.broadcasted_iota(jnp.int32, (TOK, TOK), 1)
+        row = lax.broadcasted_iota(jnp.int32, (HALF, HALF), 0)
+        col = lax.broadcasted_iota(jnp.int32, (HALF, HALF), 1)
         order = (row <= col) if upper else (row >= col)
         tri = jnp.where(jnp.logical_and(order, row // CH == col // CH), 1.0, 0.0).astype(bf16)
         first = low(v)
@@ -529,43 +540,48 @@
         third = low(rest - wide(second))
         return dot(tri, first) + (dot(tri, second) + dot(tri, third))
 
-    def forward(l, i, x_ref, out_ref, hooks):
-        hooks[0]()
-        small_whole(l)
-        xin = wide(x_ref[...])
-        normed[l] = low(xin * rms_scale(xin) * rows_of[l, 0:1])
-        nrm = normed[l]
-        qkvg[l] = dot(nrm, weight(l, QKVG))
-        rank[l] = low(dot(nrm, weight(l, SMALL)))
-        pre = dot(rank[l], rank_up[l]) + bias[l]
+    def attention(l, h, i, x_ref):
+        r = of(h)
+        xin = wide(x_ref[r])
+        nrm = low(xin * rms_scale(xin) * rows_of[l, 0:1])
+        normed[l, r] = nrm
+        qkvg[l, r] = dot(nrm, weight(l, QKVG))
+        ranked = low(dot(nrm, weight(l, SMALL)))
+        rank[l, r] = ranked
+        pre = dot(ranked, rank_up[l]) + bias[l]
         soft = jnp.log1p(jnp.exp(-jnp.abs(pre)))
-        slope[l] = jax.nn.sigmoid(-pre) / 16.0
-        cum[l] = running((jnp.minimum(pre, 0.0) - soft) / 16.0, False)
-        mixer_forward(l)
-        at = attn[l]
-        g = qkvg[l, :, 512:768]
+        slope[l, r] = jax.nn.sigmoid(-pre) / 16.0
+        cum[l, r] = running((jnp.minimum(pre, 0.0) - soft) / 16.0, False)
+        mixer_forward(l, h)
+        at = attn[l, r]
+        g = qkvg[l, r, 512:768]
         head = lax.rsqrt(jnp.mean(at * at, axis=-1, keepdims=True) + head_floor)
-        mixed[l] = low(at * head * gain[l] * g * jax.nn.sigmoid(g))
-        hooks[1]()
-        sum_start(i, dot_back(mixed[l], weight(l, OUT)))
-        hidden = wide(x_ref[rows(t)]) + sum_wait(i)
-        hid[l] = hidden
-        share_start(i + 1, nm.at[l], hidden * rms_scale(hidden) * rows_of[l, 1:2])
-        hooks[2]()
-        w_gu = weight(l, GU)
-        share_wait(i + 1, nm.at[l])
-        acts = dot(nm[l], w_gu)
-        gu[l] = acts
+        both = low(at * head * gain[l] * g * jax.nn.sigmoid(g))
+        mixed[l, r] = both
+        sum_start(i, h, dot_back(both, weight(l, OUT)))
+
+    def middle(l, h, i, x_ref):
+        hidden = wide(x_ref[rows(t, h)]) + sum_wait(i, h)
+        hid[l, h] = hidden
+        share_start(i + 1, h, nm.at[l], hidden * rms_scale(hidden) * rows_of[l, 1:2])
+
+    def feed(l, h, i):
+        share_wait(i + 1, h, nm.at[l])
+        r = of(h)
+        acts = dot(nm[l, r], weight(l, GU))
+        gu[l, r] = acts
         first = jax.nn.silu(acts[:, :FFM]) * acts[:, FFM : 2 * FFM]
         both = acts[:, 2 * FFM :]
-        lane = lax.broadcasted_iota(jnp.int32, (TOK, 128), 1)
+        lane = lax.broadcasted_iota(jnp.int32, (HALF, 128), 1)
         last = jnp.where(lane < 64, jax.nn.silu(both) * pltpu.roll(both, 64, 1), 0.0)
-        inner[l, :, :FFM] = low(first)
-        inner[l, :, FFM:] = low(last)
-        sum_start(i + 2, dot_back(inner[l], weight(l, DOWN)))
-        hooks[3]()
-        y = hid[l] + sum_wait(i + 2)
-        share_start(i + 3, out_ref, y)
+        inner[l, r, :FFM] = low(first)
+        inner[l, r, FFM:] = low(last)
+
+    def forward_down(l, h, i):
+        sum_start(i + 2, h, dot_back(inner[l, of(h)], weight(l, DOWN)))
+
+    def forward_end(l, h, i, out_ref):
+        share_start(i + 3, h, out_ref, hid[l, h] + sum_wait(i + 2, h))
 
     def silu_parts(v):
         sig = jax.nn.sigmoid(v)
@@ -579,66 +595,116 @@
                 dot_grad(left[:, a * step : (a + 1) * step], right)
             ).reshape(Z, 2, H, n)
 
-    def mixer_backward(l):
-        at = attn[l]
-        g = qkvg[l, :, 512:768]
+    def mixer_backward(l, h, dm):
+        r = of(h)
+        at = attn[l, r]
+        g = qkvg[l, r, 512:768]
         head = lax.rsqrt(jnp.mean(at * at, axis=-1, keepdims=True) + head_floor)
         unit = at * head
         act, act_slope = silu_parts(g)
-        dm = dmix[...]
-        dqkvg[:, 512:768] = low(dm * unit * gain[l] * act_slope)
+        dqkvg[r, 512:768] = low(dm * unit * gain[l] * act_slope)
         du = dm * act
         d_gain = jnp.sum(du * unit, axis=0, keepdims=True)
         w = du * gain[l]
         do = low(head * (w - unit * jnp.mean(w * unit, axis=-1, keepdims=True)))
-        q, k = qkvg[l, :, 0:128], qkvg[l, :, 128:256]
-        b = cum[l]
+        q, k = qkvg[l, r, 0:128], qkvg[l, r, 128:256]
+        b = cum[l, r]
         grow, shrink = jnp.exp(b), jnp.exp(-b)
         qd = low(q * scale * grow)
         kd = low(k * shrink)
-        v = low(qkvg[l, :, 256:512])
-        d_scores = low(jnp.where(allowed[...] > 0.0, dot_back(do, v), 0.0))
+        v = low(qkvg[l, r, 256:512])
+        d_scores = low(jnp.where(allowed[r, r] > 0.0, dot_back(do, v), 0.0))
         d_qd = dot(d_scores, kd)
         d_kd = dot_grad(d_scores, qd)
-        d_v = dot_grad(amat[l], do)
+        d_v = dot_grad(amat[l, h], do)
         d_b = wide(qd) * d_qd - wide(kd) * d_kd
         d_k = d_kd * shrink
-        out_q, out_k, out_v, out_b = [None] * BLOCKS, [None] * BLOCKS, [None] * BLOCKS, [None] * BLOCKS
-        d_state = None
-        for n in reversed(range(BLOCKS)):
-            dq_n, dk_n, dv_n, db_n = sub(d_qd, n), sub(d_k, n), sub(d_v, n), sub(d_b, n)
+        ax = aux[r]
+        per = HALF // CH
+        out_q, out_k, out_v, out_b = [None] * per, [None] * per, [None] * per, [None] * per
+        for e in reversed(range(per)):
+            n = h * per + e
+            dq_n, dk_n, dv_n, db_n = sub(d_qd, e), sub(d_k, e), sub(d_v, e), sub(d_b, e)
             if n < BLOCKS - 1:
-                bn = sub(b, n)
+                d_state = d_states[...]
+                bn = sub(b, e)
                 last = bn[CH - 1 : CH]
-                fade = jnp.exp(last - bn) * sub(aux[...], n)[:, 1:2]
-                kt = low(sub(k, n) * fade)
+                fade = jnp.exp(last - bn) * sub(ax, e)[:, 1:2]
+                kt = low(sub(k, e) * fade)
                 d_low = low(d_state)
-                d_kt = dot(sub(v, n), d_low)
+                d_kt = dot(sub(v, e), d_low)
                 dv_n = dv_n + dot_back(kt, d_low)
                 dk_n = dk_n + d_kt * fade
                 moved = wide(kt) * d_kt
                 db_n = db_n - moved
                 d_last = jnp.sum(moved, axis=0, keepdims=True)
                 if n > 0:
-                    keep = aux[n * CH : n * CH + 1, 2:3] * jnp.exp(last)
-                    d_last = d_last + keep * jnp.sum(
-                        states[l, n - 1] * d_state, axis=0, keepdims=True
-                    )
+                    keep = sub(ax, e)[0:1, 2:3] * jnp.exp(last)
+                    d_last = d_last + keep * jnp.sum(states[l, n - 1] * d_state, axis=0, keepdims=True)
                 place = lax.broadcasted_iota(jnp.int32, (CH, HK), 0)
                 db_n = db_n + jnp.where(place == CH - 1, d_last, 0.0)
             if n > 0:
-                do_n = low(wide(sub(do, n)) * sub(aux[...], n)[:, 0:1])
+                do_n = low(wide(sub(do, e)) * sub(ax, e)[:, 0:1])
                 d_across = dot(do_n, low(states[l, n - 1]))
                 dq_n = dq_n + d_across
-                db_n = db_n + wide(sub(qd, n)) * d_across
-                fresh = dot_grad(do_n, sub(qd, n))
-                d_state = fresh if n == BLOCKS - 1 else keep * d_state + fresh
-            out_q[n], out_k[n], out_v[n], out_b[n] = dq_n, dk_n, dv_n, db_n
-        dqkvg[:, 0:128] = low(jnp.concatenate(out_q, axis=0) * scale * grow)
-        dqkvg[:, 128:256] = low(jnp.concatenate(out_k, axis=0))
-        dqkvg[:, 256:512] = low(jnp.concatenate(out_v, axis=0))
+                db_n = db_n + wide(sub(qd, e)) * d_across
+                fresh = dot_grad(do_n, sub(qd, e))
+                d_states[...] = fresh if n == BLOCKS - 1 else keep * d_state + fresh
+            out_q[e], out_k[e], out_v[e], out_b[e] = dq_n, dk_n, dv_n, db_n
+        dqkvg[r, 0:128] = low(jnp.concatenate(out_q, axis=0) * scale * grow)
+        dqkvg[r, 128:256] = low(jnp.concatenate(out_k, axis=0))
+        dqkvg[r, 256:512] = low(jnp.concatenate(out_v, axis=0))
         d_decay = running(jnp.concatenate(out_b, axis=0), True)
-        return low(d_decay * slope[l]), d_gain
+        d_pre[r] = low(d_decay * slope[l, r])
+        return d_gain
+
+    def feed_back(l, h, i, dy_ref):
+        r = of(h)
+        d_inner = dot(dy_ref[r], weight(l, DOWN))
+        gate, up, both = gu[l, r, :FFM], gu[l, r, FFM : 2 * FFM], gu[l, r, 2 * FFM :]
+        act, act_slope = silu_parts(gate)
+        act_b, slope_b = silu_parts(both)
+        rest = d_inner[:, FFM:]
+        mix_b = rest * pltpu.roll(both, 64, 1) * slope_b + pltpu.roll(rest * act_b, 64, 1)
+        part = jnp.concatenate(
+            [low(d_inner[:, :FFM] * up * act_slope), low(d_inner[:, :FFM] * act), low(mix_b)], axis=1
+        )
+        d_gu[r] = part
+        sum_start(i, h, dot_back(part, weight(l, GU)))
+
+    def middle_back(l, h, i, dy_ref):
+        d_mid = sum_wait(i, h)
+        hidden = hid[l, h]
+        scale_mid = rms_scale(hidden)
+        unit = hidden * scale_mid
+        small_rows[l, 1:2] += jnp.sum(d_mid * unit, axis=0, keepdims=True)
+        scaled = d_mid * rows_of[l, 1:2]
+        d_hidden = wide(dy_ref[rows(t, h)]) + scale_mid * (
+            scaled - unit * jnp.mean(scaled * unit, axis=-1, keepdims=True)
+        )
+        d_hid[h] = d_hidden
+        share_start(i + 1, h, dh, d_hidden)
+
+    def attention_back(l, h, i, x_ref):
+        r = of(h)
+        share_wait(i + 1, h, dh)
+        d_gain = mixer_backward(l, h, dot(dh[r], weight(l, OUT)))
+        ranked = low(dot_back(d_pre[r], rank_up[l]))
+        d_rank[r] = ranked
+        partial = dot_back(dqkvg[r], weight(l, QKVG)) + dot_back(ranked, weight(l, SMALL))
+        sum_start(i + 2, h, partial)
+        xin = wide(x_ref[r])
+        small_rows[l, 0:1] += jnp.sum(partial * (xin * rms_scale(xin)), axis=0, keepdims=True)
+        return d_gain
+
+    def backward_end(l, h, i, x_ref, out_ref):
+        d_normed = sum_wait(i + 2, h)
+        xin = wide(x_ref[rows(t, h)])
+        scale_in = rms_scale(xin)
+        unit = xin * scale_in
+        scaled = d_normed * rows_of[l, 0:1]
+        dx = d_hid[h] + scale_in * (scaled - unit * jnp.mean(scaled * unit, axis=-1, keepdims=True))
+        share_start(i + 3, h, out_ref, dx)
 
     def small_copy(l, k):
         peer = (t + k) % T
@@ -646,17 +712,17 @@
             EG.at[l, :, :, peer], EB.at[l, k - 1], u_sem.at[l, 0, k - 1], u_sem.at[l, 1, k - 1], tensor=peer
         )
 
-    def small_gradients(l, d_rank, d_pre, d_gain):
+    def small_gradients(l, d_gain):
         rank_rows = downs((16, HV))
         at_gain = low(jnp.where(rank_rows == 2, d_gain, 0.0))
-        d_bias = jnp.sum(wide(d_pre), axis=0, keepdims=True)
+        d_bias = jnp.sum(wide(d_pre[...]), axis=0, keepdims=True)
         at_bias = low(jnp.where(downs((16, HK)) == 3, d_bias, 0.0))
         found = small_rows[l] + dot_back(at_gain, pick_gain[...]) + dot_back(at_bias, pick_bias[...])
         pick = low(jnp.where(lanes((16, 128)) == downs((16, 128)) + AT_IN, 1.0, 0.0))
-        ups = dot_grad(rank[l], d_pre)
+        ups = dot_grad(rank[l], d_pre[...])
         right = lanes((128, 128)) >= 64
         every = (
-            dot_grad(normed[l], d_rank)
+            dot_grad(normed[l], d_rank[...])
             + dot_grad(low(found), pick)
             + dot_grad(pick_up[0], low(jnp.where(right, pltpu.roll(ups, 64, 1), 0.0)))
             + dot_grad(pick_up[1], low(jnp.where(right, ups, 0.0)))
@@ -729,6 +795,7 @@
             [low(d_inner[:, :FFM] * up * act_slope), low(d_inner[:, :FFM] * act), low(mix_b)], axis=1
         )
         sum_start(i, dot_back(d_gu, weight(l, GU)))
+        hooks[4]()
         put(DOWN, dy, inner[l])
         scatter_swap(l, 1)
         put(GU, nm[l], d_gu)
@@ -744,14 +811,16 @@
         d_hidden = wide(dy_ref[rows(t)]) + scale_mid * (
             scaled - unit * jnp.mean(scaled * unit, axis=-1, keepdims=True)
         )
-        hid[l] = d_hidden
+        d_hid[...] = d_hidden
         share_start(i + 1, dh, d_hidden)
         hooks[1]()
         share_wait(i + 1, dh)
         dmix[...] = dot(dh[...], weight(l, OUT))
+        hooks[5]()
         d_pre, d_gain = mixer_backward(l)
         d_rank = low(dot_back(d_pre, rank_up[l]))
         partial = dot_back(dqkvg[...], weight(l, QKVG)) + dot_back(d_rank, weight(l, SMALL))
+        hooks[6]()
         sum_start(i + 2, partial)
         xin = wide(x_ref[...])
         small_rows[l, 0:1] = jnp.sum(partial * (xin * rms_scale(xin)), axis=0, keepdims=True)
@@ -768,24 +837,21 @@
         scale_in = rms_scale(xin)
         unit = xin * scale_in
         scaled = d_normed * rows_of[l, 0:1]
-        dx = hid[l] + scale_in * (scaled - unit * jnp.mean(scaled * unit, axis=-1, keepdims=True))
+        dx = d_hid[...] + scale_in * (scaled - unit * jnp.mean(scaled * unit, axis=-1, keepdims=True))
         share_start(i + 3, out_ref, dx)
 
-    def nothing():
-        pass
-
-    early, late = (6, 0, 1), (2, 3, 4, 5)
+    early, late = (0, 1, 7, 2), (3, 4, 5, 6)
 
     def first_weights():
         prepare()
-        small_swap()
         got_w.wait_recv()
         keep_w.wait()
-        for j in early[1:]:
+        for j in (0, 1, 2):
             gather_first(0, j)
+        small_swap()
         got_e.wait_recv()
         keep_e.wait()
-        gather_first(0, early[0])
+        gather_first(0, 7)
         for j in early:
             gather_second(0, j)
         for j in late:
@@ -802,75 +868,109 @@
 
         return run
 
+    small_rows[...] = jnp.zeros_like(small_rows)
     got_x.wait_recv()
     keep_x.wait()
     everything = early + late
-    forward(
-        0,
-        0,
-        xbuf.at[0],
-        x1,
-        (
-            first_weights,
-            each(gather_third, 0, late),
-            each(gather_first, 1, everything),
-            each(gather_second, 1, everything),
-        ),
-    )
-    each(gather_third, 1, everything)()
-    share_wait(3, x1)
-    forward(1, 4, x1, res.at[1], (nothing, nothing, nothing, nothing))
-
-    def send_y():
-        share_wait(7, res.at[1])
+    ahead, back = (0, 1), (1, 0)
+    x0, cot = xbuf.at[0], xbuf.at[1]
+
+    first_weights()
+    small_whole(0)
+    for h in ahead:
+        attention(0, h, 0, x0)
+    each(gather_third, 0, late[:2])()
+    for h in ahead:
+        middle(0, h, 0, x0)
+    each(gather_third, 0, late[2:])()
+    each(gather_first, 1, everything)()
+    for h in ahead:
+        feed(0, h, 0)
+        forward_down(0, h, 0)
+    each(gather_second, 1, everything)()
+    for h in ahead:
+        forward_end(0, h, 0, x1)
+    each(gather_third, 1, early)()
+    small_whole(1)
+    for h in ahead:
+        share_wait(3, h, x1)
+        attention(1, h, 4, x1)
+    each(gather_third, 1, late)()
+    for h in ahead:
+        middle(1, h, 4, x1)
+    for h in ahead:
+        feed(1, h, 4)
 
     ff, mix = (0, 1), (2, 3, 4)
-    backward(
-        1,
-        8,
-        x1,
-        xbuf.at[1],
-        dy0,
-        (
-            send_y,
-            each(scatter_first, 1, ff),
-            each(scatter_second, 1, ff),
-            each(scatter_third, 1, ff),
-        ),
-    )
+    for h in back:
+        feed_back(1, h, 8, cot)
+    for h in back:
+        forward_down(1, h, 4)
+    put(DOWN, cot[...], inner[1])
+    scatter_swap(1, 1)
+    for h in back:
+        middle_back(1, h, 8, cot)
+    put(GU, nm[1], d_gu[...])
+    scatter_swap(1, 0)
+    for h in back:
+        forward_end(1, h, 4, res.at[1])
+    d_gain = [attention_back(1, h, 8, x1) for h in back]
+    each(scatter_first, 1, ff)()
+    put(OUT, dh[...], mixed[1])
+    scatter_swap(1, 2)
+    put(QKVG, normed[1], dqkvg[...])
+    scatter_swap(1, 3)
+    scatter_swap(1, 4)
+    for h in back:
+        backward_end(1, h, 8, x1, dy0)
+    small_gradients(1, d_gain[0] + d_gain[1])
+    each(scatter_second, 1, ff)()
+    for h in back:
+        share_wait(11, h, dy0)
+        feed_back(0, h, 12, dy0)
     each(scatter_first, 1, mix)()
-    share_wait(11, dy0)
-
-    def in_second():
-        each(scatter_first, 0, ff)()
-        each(scatter_third, 1, mix)()
-        small_sum(1)
-
-    backward(
-        0,
-        12,
-        xbuf.at[0],
-        dy0,
-        res.at[0],
-        (each(scatter_second, 1, mix), in_second, each(scatter_second, 0, ff), each(scatter_third, 0, ff)),
-    )
+    each(scatter_third, 1, ff)()
+    put(DOWN, dy0[...], inner[0])
+    scatter_swap(0, 1)
+    for h in back:
+        middle_back(0, h, 12, dy0)
+    put(GU, nm[0], d_gu[...])
+    scatter_swap(0, 0)
+    each(scatter_second, 1, mix)()
+    d_gain = [attention_back(0, h, 12, x0) for h in back]
+    each(scatter_first, 0, ff)()
+    put(OUT, dh[...], mixed[0])
+    scatter_swap(0, 2)
+    put(QKVG, normed[0], dqkvg[...])
+    scatter_swap(0, 3)
+    scatter_swap(0, 4)
+    for h in back:
+        backward_end(0, h, 12, x0, res.at[0])
+    small_gradients(0, d_gain[0] + d_gain[1])
+    small_sum(1)
+    for h in back:
+        share_wait(7, h, res.at[1])
+    each(scatter_third, 1, mix)()
+    each(scatter_second, 0, ff)()
     each(scatter_first, 0, mix)()
     small_sum(0)
     small_swap_out.start()
-    share_wait(15, res.at[0])
-    give_end = remote(res.at[o], res_in, e_sem.at[0], e_sem.at[1], section=o)
+    for h in back:
+        share_wait(15, h, res.at[0])
+    each(scatter_third, 0, ff)()
+    give_end = remote(res.at[o], ends.at[0, c], e_sem.at[0], e_sem.at[1], section=o)
+    got_end = remote(res.at[o], ends.at[0, o], e_sem.at[0], e_sem.at[1], section=o)
     give_end.start()
     small_first()
     each(scatter_second, 0, mix)()
     small_second()
-    ends[0, c] = wide(res[c])
+    ends[0, c] = res[c]
     each(scatter_third, 0, mix)()
     give_grad = remote(RF.at[o], og.at[c], e_sem.at[2], e_sem.at[3], section=o)
     got_grad = remote(RF.at[o], og.at[o], e_sem.at[2], e_sem.at[3], section=o)
     give_grad.start()
     og[c] = RF[c]
-    give_end.wait_recv()
-    ends[0, o] = wide(res_in[...])
+    got_end.wait_recv()
     small_third()
     got_grad.wait_recv()
     whole = lambda c0, n: og[:, :, c0 : c0 + n].reshape(R, n)
@@ -878,13 +978,13 @@
     g_key[0] = whole(128, 128)
     g_value[0] = whole(256, 256)
     g_out_gate[0] = whole(512, 256)
-    g_out[0] = whole(*OUT).T
+    g_out[0] = whole(*OUT)
     g_gate[0, :, :FFM] = whole(GU[0], FFM)
     g_up[0, :, :FFM] = whole(GU[0] + FFM, FFM)
     both = whole(GU[0] + 2 * FFM, 128)
     g_gate[0, :, FFM:] = both[:, 0:64]
     g_up[0, :, FFM:] = pltpu.roll(both, 64, 1)[:, 0:64]
-    g_down[0] = whole(*DOWN).T[0:FFD]
+    g_down[0] = whole(*DOWN)[:, 0:FFD]
     give_end.wait_send()
     give_grad.wait_send()
     swap_w.wait_send()
@@ -928,20 +1028,20 @@
         pltpu.VMEM((2, TOK, 768), f32),
         pltpu.VMEM((2, TOK, HK), f32),
         pltpu.VMEM((2, TOK, HK), f32),
-        pltpu.VMEM((2, TOK, TOK), bf16),
+        pltpu.VMEM((2, 2, TOK // 2, TOK // 2), bf16),
         pltpu.VMEM((2, BLOCKS - 1, HV, HK), f32),
         pltpu.VMEM((2, TOK, HV), f32),
         pltpu.VMEM((2, TOK, HV), bf16),
-        pltpu.VMEM((2, TL, D), f32),
+        pltpu.VMEM((2, 2, TL // 2, D), f32),
+        pltpu.VMEM((2, TL // 2, D), f32),
         pltpu.VMEM((2, TOK, GU[1]), f32),
         pltpu.VMEM((2, TOK, DOWN[1]), bf16),
         pltpu.VMEM((2, TOK, 128), bf16),
         pltpu.VMEM((TOK, D), bf16),
         pltpu.VMEM((TOK, D), bf16),
         pltpu.VMEM((2, TOK, D), bf16),
-        pltpu.VMEM((TOK, D), bf16),
         pltpu.VMEM((2, TOK, D), bf16),
-        pltpu.VMEM((2, T - 1, TL, D), bf16),
+        pltpu.VMEM((3, 2, T - 1, TL // 2, D), bf16),
         pltpu.VMEM((X, Z, 2, H, SMALL[0]), bf16),
         pltpu.VMEM((2, X, Z, H, SMALL[0]), bf16),
         pltpu.VMEM((2, top - 1, top, H, SMALL[0]), bf16),
@@ -950,7 +1050,10 @@
         pltpu.VMEM((2, H, SMALL[0]), f32),
         pltpu.VMEM((2, H, SMALL[0]), f32),
         pltpu.VMEM((TOK, 768), bf16),
-        pltpu.VMEM((TOK, HV), f32),
+        pltpu.VMEM((TOK, GU[1]), bf16),
+        pltpu.VMEM((TOK, 128), bf16),
+        pltpu.VMEM((TOK, 128), bf16),
+        pltpu.VMEM((HV, HK), f32),
         pltpu.VMEM((2, 16, D), f32),
         pltpu.VMEM((2, X, Z, T, B, 128), bf16),
         pltpu.VMEM((2, X, Z, B, 128), bf16),
@@ -962,8 +1065,8 @@
         pltpu.SemaphoreType.DMA((9,)),
         pltpu.SemaphoreType.DMA((2, len(GATHER), 7)),
         pltpu.SemaphoreType.DMA((2, len(GATHER), 7)),
-        pltpu.SemaphoreType.DMA((16, T - 1)),
-        pltpu.SemaphoreType.DMA((16, T - 1)),
+        pltpu.SemaphoreType.DMA((16, 2, T - 1)),
+        pltpu.SemaphoreType.DMA((16, 2, T - 1)),
         pltpu.SemaphoreType.DMA((2, len(SCATTER), 7)),
         pltpu.SemaphoreType.DMA((2, len(SCATTER), 7)),
         pltpu.SemaphoreType.DMA((4,)),
@@ -971,13 +1074,16 @@
         pltpu.SemaphoreType.DMA((2, 2, T - 1)),
         pltpu.SemaphoreType.DMA((7, 2)),
     ]
+    flipped = lambda a: a.transpose(0, 2, 1)
+    operands = list(operands)
+    operands[11], operands[15] = flipped(operands[11]), flipped(operands[15])
     order = (2, 3, 4, 5, 6, 7, 8, 9, 10, 11, 12, 13, 14, 15)
-    outs = (jax.ShapeDtypeStruct((1, 2, TOK, D), f32),) + tuple(
+    outs = (jax.ShapeDtypeStruct((1, 2, TOK, D), bf16),) + tuple(
         jax.ShapeDtypeStruct(operands[k].shape, f32) for k in order
     )
     vmem = pl.BlockSpec(memory_space=pltpu.VMEM)
     smem = pl.BlockSpec(memory_space=pltpu.SMEM)
-    return pl.pallas_call(
+    results = pl.pallas_call(
         functools.partial(kernel, X, Z, T),
         out_shape=outs,
         in_specs=[vmem, smem] + [vmem] * (len(operands) - 2),
@@ -987,6 +1093,10 @@
             collective_id=0, has_side_effects=True, vmem_limit_bytes=64 * 1024 * 1024 - 65536
         ),
     )(*operands)
+    results = list(results)
+    results[0] = results[0].astype(f32)
+    results[10], results[14] = flipped(results[10]), flipped(results[14])
+    return tuple(results)
 
 
 def solution(mesh):

time: 223 us -> 189 us (0.85)
  Pallas kernels: 205 us -> 177 us
  local copies, waits for them, and re-layouts: 16.9 us -> 8.36 us
  other arithmetic: 0 us -> 2.89 us
    pallas_call x1, Pallas kernels: 205 us -> 177 us  [on_device(): pl.pallas_call(functools.partial(kernel, X, Z, T), out_shape=outs, in_spe...]
    unnamed x39 -> x42, local copies, waits for them, and re-layouts: 13.5 us -> 8.36 us
    pallas_call x2 -> x0, local copies, waits for them, and re-layouts: 3.43 us -> none  [on_device(): pl.pallas_call(functools.partial(kernel, X, Z, T), out_shape=outs, in_spe...]
    convert_element_type x0 -> x1, other arithmetic: none -> 2.89 us  [on_device(): results[0] = results[0].astype(f32)]
where the time goes in v2:
time: 189 us
  Pallas kernels  177 us (94%)
  local copies, waits for them, and re-layouts  8.36 us (4%)
  other arithmetic  2.89 us (2%)
    pallas_call x1, Pallas kernels, on_device(): pl.pallas_call(functools.partial(kernel, X, Z, T), out_shape=outs, in_spe...  177 us
    unnamed x42, local copies, waits for them, and re-layouts  8.36 us

profile of v2, /device:TPU:1, one launch (start us, length us, event | category | flops | bytes accessed | tf_op | source)
XLA Modules:
  0.0 189.1 jit_solution(12463110476990572808)
XLA Ops:
  0.7 177.0 %shard_map.271 = (bf16[1,2,256,1024]{3,2,1,0:T(8,128)(2,1)}, f32[1,16]{1,0:T(1,128)}, f32[1,64,128]{2,1,0:T(8,128)}, f32[1,64,128]{2,1,0:T(8,128)}, f32[1,64,256...) custom-call(bf16[1,2,256,1024]{3,2,1,0:T(8,128)(2,1)} %pipe_in.1, ...), custom_call_target="tpu_custom_call" | custom-call | tf_op jit(solution)/shard_map/pallas_call | solution.py:1086
  177.7 0.0 copy-start.13
  177.7 0.0 copy-start.7
  177.7 0.0 copy-start.6
  177.7 0.0 copy-start.5
  177.7 0.0 copy-start.4
  177.7 0.0 copy-start.8
  177.7 0.0 copy-start.12
  177.8 0.0 copy-start.11
  177.8 0.0 copy-start.10
  177.8 0.0 copy-start.3
  177.8 0.0 copy-start.9
  177.8 0.0 copy-start.2
  177.8 0.0 copy-start.1
  177.8 0.0 copy-start
  177.8 2.9 %convert_element_type.3 = f32[1,2,256,1024]{3,2,1,0:T(8,128)} convert(bf16[1,2,256,1024]{3,2,1,0:T(8,128)(2,1)} %get-tuple-element.30) | non-fusion elementwise | flops 524288 | bytes 3145728 | tf_op jit(solution)/shard_map/convert_element_type | solution.py:1097
  180.7 0.0 copy-done.13
  180.7 0.5 copy.45
  181.2 0.0 copy-done.7
  181.2 0.6 copy.46
  181.8 0.0 copy-done.6
  181.8 0.6 copy.47
  182.5 0.0 copy-done.5
  182.5 0.6 copy.48
  183.1 0.0 copy-done.4
  183.1 0.6 copy.49
  183.7 0.0 copy-done.8
  183.7 0.6 copy.50
  184.3 0.0 copy-done.12
  184.3 0.5 copy.51
  184.8 0.0 copy-done.11
  184.8 0.5 copy.52
  185.4 0.0 copy-done.10
  185.4 0.5 copy.53
  185.9 0.0 copy-done.3
  185.9 0.6 copy.54
  186.5 0.0 copy-done.9
  186.5 0.5 copy.55
  187.0 0.0 copy-done.2
  187.0 0.7 copy.56
  187.7 0.0 copy-done.1
  187.7 0.7 copy.57
  188.4 0.0 copy-done
  188.4 0.7 copy.58
Async XLA Ops:
  177.7 3.0 %copy-start.13 = (f32[1,16]{1,0:T(1,128)S(1)}, f32[1,16]{1,0:T(1,128)}, u32[]{:S(2)}) copy-start(f32[1,16]{1,0:T(1,128)} %get-tuple-element.61) | copy-start | bytes 196
  177.7 3.5 %copy-start.7 = (f32[1,64,128]{2,1,0:T(8,128)S(1)}, f32[1,64,128]{2,1,0:T(8,128)}, u32[]{:S(2)}) copy-start(f32[1,64,128]{2,1,0:T(8,128)} %get-tuple-element.62) | copy-start | bytes 98308
  177.7 4.1 %copy-start.6 = (f32[1,64,128]{2,1,0:T(8,128)S(1)}, f32[1,64,128]{2,1,0:T(8,128)}, u32[]{:S(2)}) copy-start(f32[1,64,128]{2,1,0:T(8,128)} %get-tuple-element.63) | copy-start | bytes 98308
  177.7 4.7 %copy-start.5 = (f32[1,64,256]{2,1,0:T(8,128)S(1)}, f32[1,64,256]{2,1,0:T(8,128)}, u32[]{:S(2)}) copy-start(f32[1,64,256]{2,1,0:T(8,128)} %get-tuple-element.64) | copy-start | bytes 196612
  177.7 5.4 %copy-start.4 = (f32[1,64,256]{2,1,0:T(8,128)S(1)}, f32[1,64,256]{2,1,0:T(8,128)}, u32[]{:S(2)}) copy-start(f32[1,64,256]{2,1,0:T(8,128)} %get-tuple-element.65) | copy-start | bytes 196612
  177.7 6.0 %copy-start.8 = (f32[1,16,16]{2,1,0:T(8,128)S(1)}, f32[1,16,16]{2,1,0:T(8,128)}, u32[]{:S(2)}) copy-start(f32[1,16,16]{2,1,0:T(8,128)} %get-tuple-element.66) | copy-start | bytes 3076
  177.7 6.6 %copy-start.12 = (f32[1,1,128]{2,1,0:T(1,128)S(1)}, f32[1,1,128]{2,1,0:T(1,128)}, u32[]{:S(2)}) copy-start(f32[1,1,128]{2,1,0:T(1,128)} %get-tuple-element.67) | copy-start | bytes 1540
  177.8 7.1 %copy-start.11 = (f32[1,8]{1,0:T(1,128)S(1)}, f32[1,8]{1,0:T(1,128)}, u32[]{:S(2)}) copy-start(f32[1,8]{1,0:T(1,128)} %get-tuple-element.68) | copy-start | bytes 100
  177.8 7.6 %copy-start.10 = (f32[1,4]{1,0:T(1,128)S(1)}, f32[1,4]{1,0:T(1,128)}, u32[]{:S(2)}) copy-start(f32[1,4]{1,0:T(1,128)} %get-tuple-element.69) | copy-start | bytes 52
  177.8 8.1 %copy-start.3 = (f32[1,64,256]{2,1,0:T(8,128)S(1)}, f32[1,64,256]{2,1,0:T(8,128)}, u32[]{:S(2)}) copy-start(f32[1,64,256]{2,1,0:T(8,128)} %get-tuple-element.40) | copy-start | bytes 196612
  177.8 8.7 %copy-start.9 = (f32[1,16]{1,0:T(1,128)S(1)}, f32[1,16]{1,0:T(1,128)}, u32[]{:S(2)}) copy-start(f32[1,16]{1,0:T(1,128)} %get-tuple-element.71) | copy-start | bytes 196
  177.8 9.2 %copy-start.2 = (f32[1,64,704]{2,1,0:T(8,128)S(1)}, f32[1,64,704]{2,1,0:T(8,128)}, u32[]{:S(2)}) copy-start(f32[1,64,704]{2,1,0:T(8,128)} %get-tuple-element.72) | copy-start | bytes 540676
  177.8 9.9 %copy-start.1 = (f32[1,64,704]{2,1,0:T(8,128)S(1)}, f32[1,64,704]{2,1,0:T(8,128)}, u32[]{:S(2)}) copy-start(f32[1,64,704]{2,1,0:T(8,128)} %get-tuple-element.73) | copy-start | bytes 540676
  177.8 10.6 %copy-start = (f32[1,64,704]{2,1,0:T(8,128)S(1)}, f32[1,64,704]{2,1,0:T(8,128)}, u32[]{:S(2)}) copy-start(f32[1,64,704]{2,1,0:T(8,128)} %get-tuple-element.44) | copy-start | bytes 540676

commit v3 on v2

--- a/solution.py
+++ b/solution.py
@@ -15,6 +15,7 @@
 FFD = 704
 FFM = 640
 QKVG = (0, 768)
+QKV, GATES = (0, 512), (512, 256)
 OUT = (768, 256)
 GU = (1024, 1408)
 DOWN = (2432, 768)
@@ -28,23 +29,26 @@
 bf16 = jnp.bfloat16
 
 GATHER = (
-    (0, 384, 0),
-    (384, 384, 1),
-    (768, 256, 0),
+    (0, 256, 0),
+    (256, 256, 1),
+    (3200, 128, 0),
+    (512, 256, 0),
+    (768, 256, 1),
     (1024, 640, 1),
     (1664, 768, 0),
     (2432, 384, 1),
     (2816, 384, 0),
-    (3200, 128, 1),
 )
 SCATTER = (
-    (1024, 1408, 0),
-    (2432, 768, 1),
-    (768, 256, 0),
+    (1024, 640, 0),
+    (1664, 768, 1),
+    (2432, 384, 0),
+    (2816, 384, 1),
+    (768, 128, 0),
+    (896, 128, 1),
     (0, 384, 0),
     (384, 384, 1),
 )
-
 
 def dot(a, b):
     return lax.dot_general(a, b, (((1,), (0,)), ((), ())), preferred_element_type=f32)
@@ -91,20 +95,8 @@
     w_up,
     w_down,
     ends,
-    g_norm_in,
-    g_query,
-    g_key,
-    g_value,
-    g_out_gate,
-    g_rank_down,
-    g_rank_up,
-    g_rank_bias,
-    g_head_gain,
-    g_out,
-    g_norm_mid,
-    g_gate,
-    g_up,
-    g_down,
+    og,
+    small,
     W,
     shard,
     tiles,
@@ -145,7 +137,6 @@
     GC,
     Q,
     RF,
-    og,
     dqkvg,
     d_gu,
     d_pre,
@@ -207,7 +198,6 @@
     for k in range(1, T):
         pl.semaphore_signal(barrier, inc=1, device_id={"tensor": (t + k) % T}, device_id_type=MESH)
     pl.semaphore_signal(barrier, inc=1, device_id={"section": o}, device_id_type=MESH)
-    pl.semaphore_wait(barrier, X + Z + T - 2)
 
     def lanes(shape):
         return lax.broadcasted_iota(jnp.int32, shape, len(shape) - 1)
@@ -245,15 +235,35 @@
             tiles.at[source], tiles.at[source], s, r, tensor=peer
         )
 
-    for k in range(1, T):
-        tile_copy(k)[0].start()
-
     MAIN = SMALL[0]
     shard[:, 0:128] = w_query[0]
     shard[:, 128:256] = w_key[0]
     shard[:, 256:512] = w_value[0]
     shard[:, 512:768] = w_out_gate[0]
     shard[:, 768:1024] = w_out[0]
+    half = lambda h: pl.ds(pl.multiple_of(h * H, H), H)
+    near, far = pl.ds(0, GU[0]), pl.ds(GU[0], MAIN - GU[0])
+    extra = pl.ds(MAIN, SMALL[1])
+
+    def swap(cols, at):
+        s, r = a_sem.at[at], a_sem.at[at + 1]
+        give = remote(shard.at[half(o), cols], W.at[c, x, z, o, :, cols], s, r, section=o)
+        got = remote(shard.at[half(o), cols], W.at[o, x, z, c, :, cols], s, r, section=o)
+        keep = pltpu.make_async_copy(shard.at[half(c), cols], W.at[c, x, z, c, :, cols], a_sem.at[at + 2])
+        return give, got, keep
+
+    swap_x = remote(own.at[o], xbuf.at[c], a_sem.at[9], a_sem.at[10], section=o)
+    got_x = remote(own.at[o], xbuf.at[o], a_sem.at[9], a_sem.at[10], section=o)
+    keep_x = pltpu.make_async_copy(own.at[c], xbuf.at[c], a_sem.at[11])
+    swap_near, got_near, keep_near = swap(near, 0)
+    swap_far, got_far, keep_far = swap(far, 3)
+    swap_e, got_e, keep_e = swap(extra, 6)
+
+    pl.semaphore_wait(barrier, X + Z + T - 2)
+    for k in range(1, T):
+        tile_copy(k)[0].start()
+    swap_near.start()
+    keep_near.start()
     shard[:, GU[0] : GU[0] + FFM] = w_gate[0, :, :FFM]
     shard[:, GU[0] + FFM : GU[0] + 2 * FFM] = w_up[0, :, :FFM]
     shard[:, GU[0] + 2 * FFM : GU[0] + GU[1]] = jnp.concatenate(
@@ -261,31 +271,10 @@
     )
     shard[:, MAIN - 128 : MAIN] = jnp.zeros((R, 128), bf16)
     shard[:, DOWN[0] : DOWN[0] + FFD] = w_down[0]
-
-    half = lambda h: pl.ds(pl.multiple_of(h * H, H), H)
-    main = pl.ds(0, MAIN)
-    extra = pl.ds(MAIN, SMALL[1])
-    swap_w = remote(
-        shard.at[half(o), main], W.at[c, x, z, o, :, main], a_sem.at[0], a_sem.at[1], section=o
-    )
-    swap_x = remote(own.at[o], xbuf.at[c], a_sem.at[2], a_sem.at[3], section=o)
-    keep_w = pltpu.make_async_copy(shard.at[half(c), main], W.at[c, x, z, c, :, main], a_sem.at[4])
-    keep_x = pltpu.make_async_copy(own.at[c], xbuf.at[c], a_sem.at[5])
-    swap_w.start()
+    swap_far.start()
+    keep_far.start()
     swap_x.start()
-    keep_w.start()
     keep_x.start()
-    got_w = remote(
-        shard.at[half(o), main], W.at[o, x, z, c, :, main], a_sem.at[0], a_sem.at[1], section=o
-    )
-    got_x = remote(own.at[o], xbuf.at[o], a_sem.at[2], a_sem.at[3], section=o)
-    swap_e = remote(
-        shard.at[half(o), extra], W.at[c, x, z, o, :, extra], a_sem.at[6], a_sem.at[7], section=o
-    )
-    got_e = remote(
-        shard.at[half(o), extra], W.at[o, x, z, c, :, extra], a_sem.at[6], a_sem.at[7], section=o
-    )
-    keep_e = pltpu.make_async_copy(shard.at[half(c), extra], W.at[c, x, z, c, :, extra], a_sem.at[8])
 
     def small_swap():
         for k in range(1, T):
@@ -472,9 +461,7 @@
         c0, n, axis = SCATTER[j]
         s_swap(l, j).wait()
         for a in range(X):
-            G[a, :, c, :, c0 : c0 + n] = low(
-                wide(G[a, :, c, :, c0 : c0 + n]) + wide(GA[l, a, :, :, c0 : c0 + n])
-            )
+            G[a, :, c, :, c0 : c0 + n] = G[a, :, c, :, c0 : c0 + n] + GA[l, a, :, :, c0 : c0 + n]
         for k in range(1, size[axis]):
             s_first(l, j, k).start()
 
@@ -540,21 +527,23 @@
         third = low(rest - wide(second))
         return dot(tri, first) + (dot(tri, second) + dot(tri, third))
 
-    def attention(l, h, i, x_ref):
+    def attention(l, h, i, x_ref, between=()):
         r = of(h)
         xin = wide(x_ref[r])
         nrm = low(xin * rms_scale(xin) * rows_of[l, 0:1])
         normed[l, r] = nrm
-        qkvg[l, r] = dot(nrm, weight(l, QKVG))
+        qkvg[l, r, 0:512] = dot(nrm, weight(l, QKV))
         ranked = low(dot(nrm, weight(l, SMALL)))
         rank[l, r] = ranked
         pre = dot(ranked, rank_up[l]) + bias[l]
         soft = jnp.log1p(jnp.exp(-jnp.abs(pre)))
         slope[l, r] = jax.nn.sigmoid(-pre) / 16.0
         cum[l, r] = running((jnp.minimum(pre, 0.0) - soft) / 16.0, False)
+        each(gather_third, l, between)()
         mixer_forward(l, h)
         at = attn[l, r]
-        g = qkvg[l, r, 512:768]
+        g = dot(nrm, weight(l, GATES))
+        qkvg[l, r, 512:768] = g
         head = lax.rsqrt(jnp.mean(at * at, axis=-1, keepdims=True) + head_floor)
         both = low(at * head * gain[l] * g * jax.nn.sigmoid(g))
         mixed[l, r] = both
@@ -752,7 +741,7 @@
 
     def small_first():
         small_swap_out.wait()
-        ES[...] = low(wide(EY[c]) + wide(EO[...]))
+        ES[...] = EY[c] + EO[...]
         for k in range(1, X):
             small_x(k).start()
 
@@ -770,18 +759,7 @@
         for k in range(1, Z):
             small_z(k).wait()
             total = total + wide(EZ[k - 1])
-        g_rank_down[0] = total[:, 0:G_RANK]
-        turn = lanes((B, 128)) == downs((B, 128))
-        for at, ref, n in (
-            (AT_IN, g_norm_in, B),
-            (AT_MID, g_norm_mid, B),
-            (AT_GAIN, g_head_gain, n_gain),
-            (AT_BIAS, g_rank_bias, n_bias),
-        ):
-            row = jnp.sum(jnp.where(turn, total[:, at : at + 1], 0.0), axis=0, keepdims=True)
-            ref[...] = row[:, 0:n]
-        turned = pltpu.roll(total[0:8], 64, 1)[0:1]
-        g_rank_up[0] = jnp.where(lanes((1, 128)) < 64, turned, total[1:2])
+        small[...] = total
 
     def backward(l, i, x_ref, dy_ref, out_ref, hooks):
         dy = dy_ref[...]
@@ -840,26 +818,33 @@
         dx = d_hid[...] + scale_in * (scaled - unit * jnp.mean(scaled * unit, axis=-1, keepdims=True))
         share_start(i + 3, out_ref, dx)
 
-    early, late = (0, 1, 7, 2), (3, 4, 5, 6)
+    first_in, mid, late = (0, 1, 2), (3, 4), (5, 6, 7, 8)
+    early = first_in + mid
 
     def first_weights():
-        prepare()
-        got_w.wait_recv()
-        keep_w.wait()
-        for j in (0, 1, 2):
+        got_near.wait_recv()
+        keep_near.wait()
+        for j in (0, 1):
             gather_first(0, j)
         small_swap()
         got_e.wait_recv()
         keep_e.wait()
-        gather_first(0, 7)
+        gather_first(0, 2)
+        for j in mid:
+            gather_first(0, j)
+        prepare()
         for j in early:
             gather_second(0, j)
+        got_far.wait_recv()
+        keep_far.wait()
         for j in late:
             gather_first(0, j)
-        for j in early:
+        for j in first_in:
             gather_third(0, j)
         for j in late:
             gather_second(0, j)
+        for j in early:
+            gather_first(1, j)
 
     def each(step, l, which):
         def run():
@@ -869,28 +854,29 @@
         return run
 
     small_rows[...] = jnp.zeros_like(small_rows)
-    got_x.wait_recv()
-    keep_x.wait()
     everything = early + late
     ahead, back = (0, 1), (1, 0)
     x0, cot = xbuf.at[0], xbuf.at[1]
 
     first_weights()
     small_whole(0)
-    for h in ahead:
-        attention(0, h, 0, x0)
+    got_x.wait_recv()
+    keep_x.wait()
+    attention(0, 0, 0, x0, mid)
+    attention(0, 1, 0, x0)
+    middle(0, 0, 0, x0)
     each(gather_third, 0, late[:2])()
-    for h in ahead:
-        middle(0, h, 0, x0)
+    middle(0, 1, 0, x0)
     each(gather_third, 0, late[2:])()
-    each(gather_first, 1, everything)()
+    each(gather_second, 1, early)()
+    each(gather_first, 1, late)()
     for h in ahead:
         feed(0, h, 0)
         forward_down(0, h, 0)
-    each(gather_second, 1, everything)()
+    each(gather_third, 1, early)()
+    each(gather_second, 1, late)()
     for h in ahead:
         forward_end(0, h, 0, x1)
-    each(gather_third, 1, early)()
     small_whole(1)
     for h in ahead:
         share_wait(3, h, x1)
@@ -901,26 +887,26 @@
     for h in ahead:
         feed(1, h, 4)
 
-    ff, mix = (0, 1), (2, 3, 4)
+    of_gu, of_down, of_out, of_qkvg = (0, 1), (2, 3), (4, 5), (6, 7)
+    ff, mix = of_down + of_gu, of_out + of_qkvg
     for h in back:
         feed_back(1, h, 8, cot)
     for h in back:
         forward_down(1, h, 4)
     put(DOWN, cot[...], inner[1])
-    scatter_swap(1, 1)
+    each(scatter_swap, 1, of_down)()
     for h in back:
         middle_back(1, h, 8, cot)
     put(GU, nm[1], d_gu[...])
-    scatter_swap(1, 0)
+    each(scatter_swap, 1, of_gu)()
     for h in back:
         forward_end(1, h, 4, res.at[1])
     d_gain = [attention_back(1, h, 8, x1) for h in back]
     each(scatter_first, 1, ff)()
     put(OUT, dh[...], mixed[1])
-    scatter_swap(1, 2)
+    each(scatter_swap, 1, of_out)()
     put(QKVG, normed[1], dqkvg[...])
-    scatter_swap(1, 3)
-    scatter_swap(1, 4)
+    each(scatter_swap, 1, of_qkvg)()
     for h in back:
         backward_end(1, h, 8, x1, dy0)
     small_gradients(1, d_gain[0] + d_gain[1])
@@ -931,40 +917,40 @@
     each(scatter_first, 1, mix)()
     each(scatter_third, 1, ff)()
     put(DOWN, dy0[...], inner[0])
-    scatter_swap(0, 1)
+    each(scatter_swap, 0, of_down)()
+    put(GU, nm[0], d_gu[...])
+    each(scatter_swap, 0, of_gu)()
     for h in back:
         middle_back(0, h, 12, dy0)
-    put(GU, nm[0], d_gu[...])
-    scatter_swap(0, 0)
     each(scatter_second, 1, mix)()
-    d_gain = [attention_back(0, h, 12, x0) for h in back]
     each(scatter_first, 0, ff)()
+    d_gain = [attention_back(0, 1, 12, x0)]
+    d_gain.append(attention_back(0, 0, 12, x0))
+    put(QKVG, normed[0], dqkvg[...])
+    each(scatter_swap, 0, of_qkvg)()
     put(OUT, dh[...], mixed[0])
-    scatter_swap(0, 2)
-    put(QKVG, normed[0], dqkvg[...])
-    scatter_swap(0, 3)
-    scatter_swap(0, 4)
+    each(scatter_swap, 0, of_out)()
+    small_gradients(0, d_gain[0] + d_gain[1])
+    each(scatter_first, 0, of_qkvg + of_out)()
     for h in back:
         backward_end(0, h, 12, x0, res.at[0])
-    small_gradients(0, d_gain[0] + d_gain[1])
+    each(scatter_second, 0, ff)()
     small_sum(1)
+    small_sum(0)
+    small_swap_out.start()
     for h in back:
         share_wait(7, h, res.at[1])
     each(scatter_third, 1, mix)()
-    each(scatter_second, 0, ff)()
-    each(scatter_first, 0, mix)()
-    small_sum(0)
-    small_swap_out.start()
     for h in back:
         share_wait(15, h, res.at[0])
-    each(scatter_third, 0, ff)()
     give_end = remote(res.at[o], ends.at[0, c], e_sem.at[0], e_sem.at[1], section=o)
     got_end = remote(res.at[o], ends.at[0, o], e_sem.at[0], e_sem.at[1], section=o)
     give_end.start()
+    each(scatter_second, 0, mix)()
     small_first()
-    each(scatter_second, 0, mix)()
+    ends[0, c] = res[c]
+    each(scatter_third, 0, ff)()
     small_second()
-    ends[0, c] = res[c]
     each(scatter_third, 0, mix)()
     give_grad = remote(RF.at[o], og.at[c], e_sem.at[2], e_sem.at[3], section=o)
     got_grad = remote(RF.at[o], og.at[o], e_sem.at[2], e_sem.at[3], section=o)
@@ -973,6 +959,45 @@
     got_end.wait_recv()
     small_third()
     got_grad.wait_recv()
+    give_end.wait_send()
+    give_grad.wait_send()
+    swap_near.wait_send()
+    swap_far.wait_send()
+    swap_x.wait_send()
+    swap_e.wait_send()
+    for k in range(1, T):
+        tile_copy(k)[0].wait_send()
+    for l in range(2):
+        for j, (_, _, axis) in enumerate(GATHER):
+            for k in range(1, size[axis]):
+                w_first(l, j, k)[0].wait_send()
+            for k in range(1, size[1 - axis]):
+                w_second(l, j, k)[0].wait_send()
+            w_third(l, j)[0].wait_send()
+
+
+def unpack(
+    packed_ends,
+    og,
+    small,
+    ends,
+    g_norm_in,
+    g_query,
+    g_key,
+    g_value,
+    g_out_gate,
+    g_rank_down,
+    g_rank_up,
+    g_rank_bias,
+    g_head_gain,
+    g_out,
+    g_norm_mid,
+    g_gate,
+    g_up,
+    g_down,
+):
+    R, B = 2 * og.shape[1], small.shape[0]
+    ends[...] = wide(packed_ends[...])
     whole = lambda c0, n: og[:, :, c0 : c0 + n].reshape(R, n)
     g_query[0] = whole(0, 128)
     g_key[0] = whole(128, 128)
@@ -985,20 +1010,20 @@
     g_gate[0, :, FFM:] = both[:, 0:64]
     g_up[0, :, FFM:] = pltpu.roll(both, 64, 1)[:, 0:64]
     g_down[0] = whole(*DOWN)[:, 0:FFD]
-    give_end.wait_send()
-    give_grad.wait_send()
-    swap_w.wait_send()
-    swap_x.wait_send()
-    swap_e.wait_send()
-    for k in range(1, T):
-        tile_copy(k)[0].wait_send()
-    for l in range(2):
-        for j, (_, _, axis) in enumerate(GATHER):
-            for k in range(1, size[axis]):
-                w_first(l, j, k)[0].wait_send()
-            for k in range(1, size[1 - axis]):
-                w_second(l, j, k)[0].wait_send()
-            w_third(l, j)[0].wait_send()
+    total = small[...]
+    g_rank_down[0] = total[:, 0 : g_rank_down.shape[2]]
+    lane = lax.broadcasted_iota(jnp.int32, (B, 128), 1)
+    turn = lane == lax.broadcasted_iota(jnp.int32, (B, 128), 0)
+    for at, ref in (
+        (AT_IN, g_norm_in),
+        (AT_MID, g_norm_mid),
+        (AT_GAIN, g_head_gain),
+        (AT_BIAS, g_rank_bias),
+    ):
+        row = jnp.sum(jnp.where(turn, total[:, at : at + 1], 0.0), axis=0, keepdims=True)
+        ref[...] = row[:, 0 : ref.shape[1]]
+    turned = pltpu.roll(total[0:8], 64, 1)[0:1]
+    g_rank_up[0] = jnp.where(lane[0:1] < 64, turned, total[1:2])
 
 
 def on_device(X, Z, *operands):
@@ -1048,7 +1073,6 @@
         pltpu.VMEM((2, top - 1, H, SMALL[0]), bf16),
         pltpu.VMEM((2, top, H, SMALL[0]), bf16),
         pltpu.VMEM((2, H, SMALL[0]), f32),
-        pltpu.VMEM((2, H, SMALL[0]), f32),
         pltpu.VMEM((TOK, 768), bf16),
         pltpu.VMEM((TOK, GU[1]), bf16),
         pltpu.VMEM((TOK, 128), bf16),
@@ -1062,7 +1086,7 @@
         pltpu.VMEM((X, Z, B, 128), bf16),
         pltpu.VMEM((X - 1, Z, B, 128), bf16),
         pltpu.VMEM((Z - 1, B, 128), bf16),
-        pltpu.SemaphoreType.DMA((9,)),
+        pltpu.SemaphoreType.DMA((12,)),
         pltpu.SemaphoreType.DMA((2, len(GATHER), 7)),
         pltpu.SemaphoreType.DMA((2, len(GATHER), 7)),
         pltpu.SemaphoreType.DMA((16, 2, T - 1)),
@@ -1077,24 +1101,34 @@
     flipped = lambda a: a.transpose(0, 2, 1)
     operands = list(operands)
     operands[11], operands[15] = flipped(operands[11]), flipped(operands[15])
-    order = (2, 3, 4, 5, 6, 7, 8, 9, 10, 11, 12, 13, 14, 15)
-    outs = (jax.ShapeDtypeStruct((1, 2, TOK, D), bf16),) + tuple(
-        jax.ShapeDtypeStruct(operands[k].shape, f32) for k in order
-    )
     vmem = pl.BlockSpec(memory_space=pltpu.VMEM)
     smem = pl.BlockSpec(memory_space=pltpu.SMEM)
-    results = pl.pallas_call(
+    packed = pl.pallas_call(
         functools.partial(kernel, X, Z, T),
-        out_shape=outs,
+        out_shape=(
+            jax.ShapeDtypeStruct((1, 2, TOK, D), bf16),
+            jax.ShapeDtypeStruct((2, H, SMALL[0]), f32),
+            jax.ShapeDtypeStruct((B, 128), f32),
+        ),
         in_specs=[vmem, smem] + [vmem] * (len(operands) - 2),
-        out_specs=(vmem,) * len(outs),
+        out_specs=(vmem,) * 3,
         scratch_shapes=scratch,
         compiler_params=pltpu.CompilerParams(
             collective_id=0, has_side_effects=True, vmem_limit_bytes=64 * 1024 * 1024 - 65536
         ),
     )(*operands)
-    results = list(results)
-    results[0] = results[0].astype(f32)
+    outs = (jax.ShapeDtypeStruct((1, 2, TOK, D), f32),) + tuple(
+        jax.ShapeDtypeStruct(operands[k].shape, f32) for k in range(2, 16)
+    )
+    results = list(
+        pl.pallas_call(
+            unpack,
+            out_shape=outs,
+            in_specs=[vmem] * 3,
+            out_specs=(vmem,) * len(outs),
+            compiler_params=pltpu.CompilerParams(vmem_limit_bytes=32 * 1024 * 1024),
+        )(*packed)
+    )
     results[10], results[14] = flipped(results[10]), flipped(results[14])
     return tuple(results)
 

time: 189 us -> 165 us (0.87)
  Pallas kernels: 177 us -> 161 us
  local copies, waits for them, and re-layouts: 8.36 us -> 3.06 us
  other arithmetic: 2.89 us -> 0 us
    pallas_call x1 -> x2, Pallas kernels: 177 us -> 161 us  [the longest x1 159 us: on_device(): pl.pallas_call(functools.partial(kernel, X, Z, T), out_shape=(jax.ShapeDt...]
    unnamed x42 -> x6, local copies, waits for them, and re-layouts: 8.36 us -> 3.06 us
    convert_element_type x1 -> x0, other arithmetic: 2.89 us -> none  [on_device(): results[0] = results[0].astype(f32)]
where the time goes in v3:
time: 165 us; the launch traced here: 164 us
  Pallas kernels  161 us (98%)
  local copies, waits for them, and re-layouts  3.06 us (2%)
    pallas_call x1, Pallas kernels, on_device(): pl.pallas_call(functools.partial(kernel, X, Z, T), out_shape=(jax.ShapeDt...  159 us

profile of v3, /device:TPU:1, one launch (start us, length us, event | category | flops | bytes accessed | tf_op | source)
XLA Modules:
  0.0 164.5 jit_solution(7137003256110880507)
XLA Ops:
  0.7 158.9 %shard_map.271 = (bf16[1,2,256,1024]{3,2,1,0:T(8,128)(2,1)}, f32[2,32,3200]{2,1,0:T(8,128)}, f32[16,128]{1,0:T(8,128)}) custom-call(bf16[1,2,256,1024]{3,2,1,0:T(8,128)(2,1)} %pipe_in.1, s32[2,4]{1,0:T(2,128)} %doc_lengths.1, bf16[1,16]{1,0:T(2,128)(2,1)} %norm_in.1, bf16[1,64,128]{2,1,0:T(8,128)(2,1)} %w_query.1, bf16[1,64,128]{2,1,0:T(8,128)(2,1)} %w_key.1, ...), custom_call_target="tpu_custom_call" | custom-call | tf_op jit(solution)/shard_map/pallas_call | solution.py:1106
  159.5 0.0 copy-start
  159.5 1.2 copy-done
  160.7 0.0 copy-start.1
  160.7 1.1 copy-done.1
  161.9 0.0 copy-start.2
  161.9 0.7 copy-done.2
  162.6 1.7 %shard_map.272 = (f32[1,2,256,1024]{3,2,1,0:T(8,128)}, f32[1,16]{1,0:T(1,128)}, f32[1,64,128]{2,1,0:T(8,128)}, f32[1,64,128]{2,1,0:T(8,128)}, f32[1,64,256]{2,1,...) custom-call(bf16[1,2,256,1024]{3,2,1,0:T(8,128)(2,1)S(1)} %copy-done, ...), custom_call_target="tpu_custom_call" | custom-call | tf_op jit(solution)/shard_map/pallas_call | solution.py:1124
Async XLA Ops:
  159.5 1.2 copy-start
  160.7 1.1 copy-start.1
  161.9 0.7 copy-start.2

commit v4 on v3

--- a/solution.py
+++ b/solution.py
@@ -389,23 +389,28 @@
     def of(h):
         return slice(h * HALF, (h + 1) * HALF)
 
+    def slot(i):
+        return 2 if i == 6 else i // 2 % 2
+
     def sum_copy(i, h, k):
         peer = (t + k) % T
-        into = rbuf.at[2 if i == 6 else i // 2 % 2, h, k - 1]
+        into = rbuf.at[slot(i), h, k - 1]
         return remote(
-            pbuf.at[i // 2 % 2, rows(peer, h)], into, ys.at[i, h, k - 1], yr.at[i, h, k - 1], tensor=peer
-        )
+            pbuf.at[slot(i), rows(peer, h)], into, ys.at[i, h, k - 1], yr.at[i, h, k - 1], tensor=peer
+        )
+
+    far_first = sorted(range(1, T), key=lambda k: -min(k, T - k))
 
     def sum_start(i, h, part):
-        pbuf[i // 2 % 2, of(h)] = low(part)
-        for k in range(1, T):
+        pbuf[slot(i), of(h)] = low(part)
+        for k in far_first:
             sum_copy(i, h, k).start()
 
     def sum_wait(i, h):
-        total = wide(pbuf[i // 2 % 2, rows(t, h)])
+        total = wide(pbuf[slot(i), rows(t, h)])
         for k in range(1, T):
             sum_copy(i, h, k).wait_recv()
-            total = total + wide(rbuf[2 if i == 6 else i // 2 % 2, h, k - 1])
+            total = total + wide(rbuf[slot(i), h, k - 1])
         for k in range(1, T):
             sum_copy(i, h, k).wait_send()
         return total
@@ -418,7 +423,7 @@
 
     def share_start(i, h, ref, value):
         ref[rows(t, h)] = low(value)
-        for k in range(1, T):
+        for k in far_first:
             share_copy(i, h, ref, k)[0].start()
 
     def share_wait(i, h, ref):
@@ -523,9 +528,7 @@
         tri = jnp.where(jnp.logical_and(order, row // CH == col // CH), 1.0, 0.0).astype(bf16)
         first = low(v)
         rest = v - wide(first)
-        second = low(rest)
-        third = low(rest - wide(second))
-        return dot(tri, first) + (dot(tri, second) + dot(tri, third))
+        return dot(tri, first) + dot(tri, low(rest))
 
     def attention(l, h, i, x_ref, between=()):
         r = of(h)
@@ -832,13 +835,15 @@
         gather_first(0, 2)
         for j in mid:
             gather_first(0, j)
-        prepare()
-        for j in early:
-            gather_second(0, j)
         got_far.wait_recv()
         keep_far.wait()
         for j in late:
             gather_first(0, j)
+        for j in (0, 1):
+            gather_second(0, j)
+        prepare()
+        for j in early[2:]:
+            gather_second(0, j)
         for j in first_in:
             gather_third(0, j)
         for j in late:
@@ -891,49 +896,49 @@
     ff, mix = of_down + of_gu, of_out + of_qkvg
     for h in back:
         feed_back(1, h, 8, cot)
+    put(DOWN, cot[...], inner[1])
+    each(scatter_swap, 1, of_down)()
+    middle_back(1, 1, 8, cot)
+    put(GU, nm[1], d_gu[...])
+    each(scatter_swap, 1, of_gu)()
+    middle_back(1, 0, 8, cot)
     for h in back:
         forward_down(1, h, 4)
-    put(DOWN, cot[...], inner[1])
-    each(scatter_swap, 1, of_down)()
-    for h in back:
-        middle_back(1, h, 8, cot)
-    put(GU, nm[1], d_gu[...])
-    each(scatter_swap, 1, of_gu)()
-    for h in back:
-        forward_end(1, h, 4, res.at[1])
     d_gain = [attention_back(1, h, 8, x1) for h in back]
-    each(scatter_first, 1, ff)()
     put(OUT, dh[...], mixed[1])
     each(scatter_swap, 1, of_out)()
+    backward_end(1, 1, 8, x1, dy0)
     put(QKVG, normed[1], dqkvg[...])
     each(scatter_swap, 1, of_qkvg)()
-    for h in back:
-        backward_end(1, h, 8, x1, dy0)
+    each(scatter_first, 1, ff)()
+    backward_end(1, 0, 8, x1, dy0)
     small_gradients(1, d_gain[0] + d_gain[1])
-    each(scatter_second, 1, ff)()
     for h in back:
         share_wait(11, h, dy0)
         feed_back(0, h, 12, dy0)
-    each(scatter_first, 1, mix)()
-    each(scatter_third, 1, ff)()
+    each(scatter_second, 1, ff)()
     put(DOWN, dy0[...], inner[0])
     each(scatter_swap, 0, of_down)()
+    middle_back(0, 1, 12, dy0)
     put(GU, nm[0], d_gu[...])
     each(scatter_swap, 0, of_gu)()
+    each(scatter_first, 1, mix)()
+    middle_back(0, 0, 12, dy0)
+    each(scatter_first, 0, ff)()
+    each(scatter_third, 1, ff)()
+    d_gain = []
     for h in back:
-        middle_back(0, h, 12, dy0)
+        forward_end(1, h, 4, res.at[1])
+        d_gain.append(attention_back(0, h, 12, x0))
     each(scatter_second, 1, mix)()
-    each(scatter_first, 0, ff)()
-    d_gain = [attention_back(0, 1, 12, x0)]
-    d_gain.append(attention_back(0, 0, 12, x0))
     put(QKVG, normed[0], dqkvg[...])
     each(scatter_swap, 0, of_qkvg)()
     put(OUT, dh[...], mixed[0])
     each(scatter_swap, 0, of_out)()
+    backward_end(0, 1, 12, x0, res.at[0])
+    each(scatter_first, 0, of_qkvg + of_out)()
     small_gradients(0, d_gain[0] + d_gain[1])
-    each(scatter_first, 0, of_qkvg + of_out)()
-    for h in back:
-        backward_end(0, h, 12, x0, res.at[0])
+    backward_end(0, 0, 12, x0, res.at[0])
     each(scatter_second, 0, ff)()
     small_sum(1)
     small_sum(0)
@@ -1065,7 +1070,7 @@
         pltpu.VMEM((TOK, D), bf16),
         pltpu.VMEM((TOK, D), bf16),
         pltpu.VMEM((2, TOK, D), bf16),
-        pltpu.VMEM((2, TOK, D), bf16),
+        pltpu.VMEM((3, TOK, D), bf16),
         pltpu.VMEM((3, 2, T - 1, TL // 2, D), bf16),
         pltpu.VMEM((X, Z, 2, H, SMALL[0]), bf16),
         pltpu.VMEM((2, X, Z, H, SMALL[0]), bf16),

time: 165 us -> 164 us (level)
  Pallas kernels: 161 us -> 158 us
    pallas_call x1, Pallas kernels: 159 us -> 157 us  [on_device(): pl.pallas_call(functools.partial(kernel, X, Z, T), out_shape=(jax.ShapeDt...]
where the time goes in v4:
time: 164 us; the launch traced here: 162 us
  Pallas kernels  158 us (96%)
  local copies, waits for them, and re-layouts  3.06 us (2%)
    pallas_call x1, Pallas kernels, on_device(): pl.pallas_call(functools.partial(kernel, X, Z, T), out_shape=(jax.ShapeDt...  157 us

profile of v4, /device:TPU:1, one launch (start us, length us, event | category | flops | bytes accessed | tf_op | source)
XLA Modules:
  0.0 162.3 jit_solution(10383547971908527673)
XLA Ops:
  0.7 156.7 %shard_map.271 = (bf16[1,2,256,1024]{3,2,1,0:T(8,128)(2,1)}, f32[2,32,3200]{2,1,0:T(8,128)}, f32[16,128]{1,0:T(8,128)}) custom-call(bf16[1,2,256,1024]{3,2,1,0:T(8,128)(2,1)} %pipe_in.1, s32[2,4]{1,0:T(2,128)} %doc_lengths.1, bf16[1,16]{1,0:T(2,128)(2,1)} %norm_in.1, bf16[1,64,128]{2,1,0:T(8,128)(2,1)} %w_query.1, bf16[1,64,128]{2,1,0:T(8,128)(2,1)} %w_key.1, ...), custom_call_target="tpu_custom_call" | custom-call | tf_op jit(solution)/shard_map/pallas_call | solution.py:1111
  157.3 0.0 copy-start
  157.3 1.2 copy-done
  158.6 0.0 copy-start.1
  158.6 1.1 copy-done.1
  159.7 0.0 copy-start.2
  159.7 0.7 copy-done.2
  160.4 1.7 %shard_map.272 = (f32[1,2,256,1024]{3,2,1,0:T(8,128)}, f32[1,16]{1,0:T(1,128)}, f32[1,64,128]{2,1,0:T(8,128)}, f32[1,64,128]{2,1,0:T(8,128)}, f32[1,64,256]{2,1,...) custom-call(bf16[1,2,256,1024]{3,2,1,0:T(8,128)(2,1)S(1)} %copy-done, ...), custom_call_target="tpu_custom_call" | custom-call | tf_op jit(solution)/shard_map/pallas_call | solution.py:1129
Async XLA Ops:
  157.3 1.2 copy-start
  158.6 1.1 copy-start.1
  159.7 0.7 copy-start.2
